TPU v7x, 256 devices: a whole 4x4x8 slice. The times are simulated.
256 devices in a mesh: dp: 4 (over x_lo, core), ctx: 8 (over z), head: 8 (over y, x_hi).
Axes of the slice: x: 4 (x_hi: 2, x_lo: 2; x = x_hi * 2 + x_lo), y: 4, z: 8, core: 2. Of those that a mesh axis runs over, the one named last changes fastest.
Arguments:
- query_matrix: bfloat16 [4, 2048, 8, 8, 128], P('dp', 'ctx', 'head'), may hold values from -180 to 180
- key_matrix: bfloat16 [4, 2048, 8, 128], P('dp', 'ctx', 'head'), may hold values from -6 to 6
- value_matrix: bfloat16 [4, 2048, 8, 128], P('dp', 'ctx', 'head'), may hold values from -6 to 6
- output_gradient: bfloat16 [4, 2048, 8, 8, 128], P('dp', 'ctx', 'head'), may hold values from -6 to 6
- normed_layer_input: bfloat16 [4, 2048, 8192], P('dp', 'ctx', 'head'), may hold values from -6 to 6
- adapter_down: bfloat16 [8192, 8], P('head'), may hold values from -0.0625 to 0.0625
- adapter_up: bfloat16 [8, 8, 8, 128], P(None, 'head'), may hold values from -2 to 2
- lengths: int32 [4], P('dp'), may hold values from 1024 to 2048, as said below
Outputs:
- query_gradient: bfloat16 [4, 2048, 8, 8, 128], P('dp', 'ctx', 'head')
- key_gradient: bfloat16 [4, 2048, 8, 128], P('dp', 'ctx', 'head')
- value_gradient: bfloat16 [4, 2048, 8, 128], P('dp', 'ctx', 'head')
- down_matrix_gradient: float32 [8192, 8], P('head')
- up_matrix_gradient: float32 [8, 8, 8, 128], P(None, 'head')
Inputs may be any that keep to these rules, and one draw needn't show every extreme that they name: `lengths`: each value is at least half a sequence, and some sequence is whole.
All inputs are finite; a program needn't handle non-finite values.
Results may differ from a plain program's by a relative error of at most 0.014.
Values may be sent and summed in bfloat16 or wider, within the bound.
A program may use at most 64 MiB of HBM per device.

v0:
```python
import math

import jax
import jax.numpy as jnp
from jax import lax
from jax.sharding import PartitionSpec as P

ADAPTER_SCALE = 2.0
BLOCKED = -1e30


def shortened(array):
    return jax.tree.map(lambda a: a.astype(jnp.bfloat16) if a.dtype == jnp.float32 else a, array)


def shifted_2(value, axis, steps):
    count = lax.axis_size(axis)
    pairs = [(source, (source + steps) % count) for source in range(count)]
    return lax.ppermute(value, axis, pairs)


def attend_rows(queries, keys_head, values_head, grads_head, query_pos, key_pos, length):
    query_count = queries.shape[0]
    key_count = keys_head.shape[0]
    width = queries.shape[-1]
    softmax_scale = 1.0 / math.sqrt(width)
    block_rows = min(512, query_count)
    key_index = jnp.arange(key_count, dtype=jnp.int32)
    valid_key = key_pos < length
    grad_block = grads_head
    grad_block = jnp.where(
        (query_pos < length)[:, None, None], grad_block, jnp.zeros_like(grad_block)
    )
    query_index = jnp.arange(block_rows, dtype=jnp.int32)
    scores = (
        jnp.einsum("igd,jd->gij", queries, keys_head, preferred_element_type=jnp.float32)
        * softmax_scale
    )
    allowed = (key_index[None, :] <= query_index[:, None]) & (
        valid_key[None, :] | (key_index[None, :] == query_index[:, None])
    )
    scores = jnp.where(allowed[None], scores, BLOCKED)
    row_max = jnp.max(scores, axis=-1, keepdims=True)
    weights = jnp.exp(scores - row_max)
    probs = weights / jnp.sum(weights, axis=-1, keepdims=True)
    probs_low = probs.astype(jnp.bfloat16)
    output = jnp.einsum("gij,jd->igd", probs_low, values_head, preferred_element_type=jnp.float32)
    out_dot = jnp.sum(grad_block.astype(jnp.float32) * output, axis=-1)
    prob_grad = jnp.einsum(
        "igd,jd->gij", grad_block, values_head, preferred_element_type=jnp.float32
    )
    score_grad = (probs * (prob_grad - jnp.transpose(out_dot)[:, :, None])).astype(jnp.bfloat16)
    query_grad = (
        jnp.einsum("gij,jd->igd", score_grad, keys_head, preferred_element_type=jnp.float32)
        * softmax_scale
    )
    query_parts = query_grad.astype(jnp.bfloat16)
    key_total = jnp.einsum("gij,igd->jd", score_grad, queries, preferred_element_type=jnp.float32)
    value_total = jnp.einsum(
        "gij,igd->jd", probs_low, grad_block, preferred_element_type=jnp.float32
    )
    return (query_parts, key_total, value_total)


def head_backward(queries, keys_head, values_head, grads_head, positions, length):
    softmax_scale = 1.0 / math.sqrt(queries.shape[-1])
    grad_q, key_total, value_total = attend_rows(
        queries, keys_head, values_head, grads_head, positions, positions, length
    )
    return (
        grad_q,
        (key_total * softmax_scale).astype(jnp.bfloat16),
        value_total.astype(jnp.bfloat16),
    )


def on_device(
    query_matrix,
    key_matrix,
    value_matrix,
    output_gradient,
    normed_layer_input,
    adapter_down,
    adapter_up,
    lengths,
):
    group_rows = query_matrix.shape[1]
    half_rows = group_rows // 2
    kv_local = key_matrix.shape[2]
    ctx_count = lax.axis_size("ctx")
    ctx_place = lax.axis_index("ctx")
    kv_total = kv_local * lax.axis_size("head")
    head_ids = lax.axis_index("head") * kv_local + jnp.arange(kv_local, dtype=jnp.int32)
    shifted = head_ids < kv_total // 2
    length = lengths[0]
    own_rows = (query_matrix[0], key_matrix[0], value_matrix[0], output_gradient[0])
    token_input_rows = normed_layer_input[0]
    low_rank_product = jnp.dot(token_input_rows, adapter_down, preferred_element_type=jnp.float32)
    local_pos = ctx_place * group_rows + jnp.arange(group_rows, dtype=jnp.int32)

    def head_mask(sample):
        return shifted.reshape((1, kv_local) + (1,) * (sample.ndim - 2))

    arrived = shifted_2(shortened(tuple((piece[:half_rows] for piece in own_rows))), "ctx", -1)

    def arrange(mine, theirs):
        moved = jnp.concatenate([mine[half_rows:], theirs], axis=0)
        return jnp.where(head_mask(mine), moved, mine)

    grouped = [arrange(mine, theirs) for mine, theirs in zip(own_rows, arrived)]
    next_pos = (ctx_place + 1) % ctx_count * group_rows + jnp.arange(half_rows, dtype=jnp.int32)
    moved_pos = jnp.concatenate([local_pos[half_rows:], next_pos])
    positions = jnp.where(shifted[0], moved_pos, local_pos)
    grad_q, grad_k, grad_v = head_backward(
        grouped[0][:, 0], grouped[1][:, 0], grouped[2][:, 0], grouped[3][:, 0], positions, length
    )
    query_list = [grad_q]
    key_list = [grad_k]
    value_list = [grad_v]
    results = (
        jnp.stack(query_list, axis=1),
        jnp.stack(key_list, axis=1),
        jnp.stack(value_list, axis=1),
    )
    returned = shifted_2(shortened(tuple((piece[half_rows:] for piece in results))), "ctx", 1)

    def settle(grouped_grad, coming_back):
        moved = jnp.concatenate([coming_back, grouped_grad[:half_rows]], axis=0)
        return jnp.where(head_mask(grouped_grad), moved, grouped_grad)

    query_gradient = settle(results[0], returned[0])
    key_gradient = settle(results[1], returned[1])
    value_gradient = settle(results[2], returned[2])
    flattened_gradient = query_gradient.reshape(group_rows, -1)
    flattened_up = adapter_up.reshape(adapter_up.shape[0], -1)
    grad_part = lax.dot_general(
        flattened_gradient,
        flattened_up,
        (((1,), (1,)), ((), ())),
        preferred_element_type=jnp.float32,
    )
    rank_total, grad_total = lax.psum((low_rank_product, grad_part), "head")
    low_rank_input = rank_total.astype(jnp.bfloat16)
    low_rank_gradient = grad_total.astype(jnp.bfloat16)
    up_product = ADAPTER_SCALE * lax.dot_general(
        low_rank_input,
        flattened_gradient,
        (((0,), (0,)), ((), ())),
        preferred_element_type=jnp.float32,
    )
    down_product = ADAPTER_SCALE * lax.dot_general(
        token_input_rows,
        low_rank_gradient,
        (((0,), (0,)), ((), ())),
        preferred_element_type=jnp.float32,
    )
    down_matrix_gradient, up_matrix_gradient = lax.psum((down_product, up_product), ("dp", "ctx"))
    return (
        query_gradient[None],
        key_gradient[None],
        value_gradient[None],
        down_matrix_gradient,
        up_matrix_gradient.reshape(adapter_up.shape),
    )


def solution(mesh):
    return jax.shard_map(
        on_device,
        mesh=mesh,
        in_specs=(
            P("dp", "ctx", "head", None, None),
            P("dp", "ctx", "head", None),
            P("dp", "ctx", "head", None),
            P("dp", "ctx", "head", None, None),
            P("dp", "ctx", "head"),
            P("head", None),
            P(None, "head", None, None),
            P("dp"),
        ),
        out_specs=(
            P("dp", "ctx", "head", None, None),
            P("dp", "ctx", "head", None),
            P("dp", "ctx", "head", None),
            P("head", None),
            P(None, "head", None, None),
        ),
        check_vma=False,
    )
```

profile of v0, /device:TPU:1, one launch (start us, length us, event | category | flops | bytes accessed | tf_op | source)
XLA Modules:
  0.0 309.2 jit_solution(16252999962947075106)
XLA Ops:
  7.2 1.5 slice_bitcast_fusion.8
  8.7 6.4 %collective-permute-start = (bf16[128,1,128]{2,0,1:T(8,128)(2,1)S(1)}, bf16[128,1,128]{2,0,1:T(8,128)(2,1)S(1)}, u32[]{:S(2)}, u32[]{:S(2)}) collective-permute-start(bf16[128,1,128]{2,0,1:T(8,128)(2,1)S(1)} %get-tuple-element.27), channel_id=1, source_target_pairs={{0,56},{8,0},{16,8},{24,16},{32,24},{40,32},{48,40},{56,48},{1,57}... | collective-permute-start | bytes 98312 | tf_op jit(solution)/shard_map/ppermute | solution.py:19
  15.1 1.4 fusion.88
  16.6 0.7 collective-permute-start.2
  17.3 1.3 copy.13
  18.6 0.9 slice_bitcast_fusion.10
  19.5 0.7 collective-permute-start.1
  20.6 1.0 fusion.87
  23.4 0.7 fusion.39
  24.1 2.0 collective-permute-done.1
  26.8 1.9 fusion.89
  29.0 2.8 collective-permute-done.3
  31.8 1.4 fusion.9
  33.3 1.4 fusion.6
  34.8 1.5 fusion.2
  36.8 0.8 collective-permute-start.5
  38.5 2.3 collective-permute-done.5
  41.5 3.9 %collective-permute-done.4 = bf16[128,1,8,128]{0,3,2,1:T(8,128)(2,1)S(1)} collective-permute-done((bf16[128,1,8,128]{0,3,2,1:T(8,128)(2,1)S(1)}, bf16[128,1,8,128]{0,3,2,1:T(8,128)(2,1)S(1)}, u32[]{:S(2)}, u32[]{:S(2)}) %collective-permute-start.4) | collective-permute-done | bytes 262176 | tf_op jit(solution)/shard_map/ppermute | solution.py:19
  45.8 39.9 %all-reduce.1 = (bf16[256,8]{1,0:T(8,128)(2,1)S(1)}, bf16[256,8]{1,0:T(8,128)(2,1)S(1)}) all-reduce(f32[256,8]{1,0:T(8,128)S(1)} %convolution_bitcast_fusion.1, f32[256,8]{1,0:T(8,128)S(1)} %fusion.30), channel_id=1, replica_groups=mesh['dp'=4,'ctx'=8,'head'=8] {'head'}, use_global_device_ids=true, to_apply=%region_3.4 | all-reduce | flops 4096 | bytes 24576 | tf_op jit(solution)/shard_map/psum | solution.py:142
  85.8 0.8 fusion.12
  88.2 1.1 copy.30
  89.3 210.3 %all-reduce.4.cloned.1.call-done = (f32[1024,8]{0,1:T(8,128)}, f32[8,1,8,128]{3,2,1,0:T(8,128)}) async-done(((f32[1024,8]{0,1:T(8,128)}, f32[8,1,8,128]{3,2,1,0:T(8,128)}), (f32[1024,8]{0,1:T(8,128)}, f32[8,1,8,128]{3,2,1,0:T(8,128)})) %all-reduce.4.cloned.1.call-update) | async-done | bytes 65552 | tf_op jit(solution)/shard_map/psum | solution.py:157
  299.6 1.4 copy.47
  301.0 1.4 copy.48
  (64 shorter events, 6.4 us)
Async XLA Ops:
  7.2 15.9 %copy-start = (bf16[1,256,1024]{2,1,0:T(8,128)(2,1)S(1)}, bf16[1,256,1024]{2,1,0:T(8,128)(2,1)}, u32[]{:S(2)}) copy-start(bf16[1,256,1024]{2,1,0:T(8,128)(2,1)} %param.12) | copy-start | bytes 1572868
  7.2 13.1 %copy-start.3 = (bf16[1,256,1,8,128]{4,3,2,1,0:T(8,128)(2,1)S(1)}, bf16[1,256,1,8,128]{4,3,2,1,0:T(8,128)(2,1)}, u32[]{:S(2)}) copy-start(bf16[1,256,1,8,128]{4,3,2,1,0:T(8,128)(2,1)} %param.11) | copy-start | bytes 1572868
  7.2 292.4 %all-reduce.4.cloned.1.call-start = ((), (), s32[]{:S(2)}) async-start(), calls=%async_computation | async-start | bytes 131072 | tf_op jit(solution)/shard_map/psum | solution.py:157
  8.7 15.4 %collective-permute-start = (bf16[128,1,128]{2,0,1:T(8,128)(2,1)S(1)}, bf16[128,1,128]{2,0,1:T(8,128)(2,1)S(1)}, u32[]{:S(2)}, u32[]{:S(2)}) collective-permute-start(bf16[128,1,128]{2,0,1:T(8,128)(2,1)S(1)} %get-tuple-element.27), channel_id=1, source_target_pairs={{0,56},{8,0},{16,8},{24,16},{32,24},{40,32},{48,40},{56,48},{1,57}... | collective-permute-start | bytes 98312 | tf_op jit(solution)/shard_map/ppermute | solution.py:19
  16.6 16.7 %collective-permute-start.2 = (bf16[128,1,128]{2,0,1:T(8,128)(2,1)}, bf16[128,1,128]{2,0,1:T(8,128)(2,1)}, u32[]{:S(2)}, u32[]{:S(2)}) collective-permute-start(bf16[128,1,128]{2,0,1:T(8,128)(2,1)} %get-tuple-element.31), channel_id=1, source_target_pairs={{0,56},{8,0},{16,8},{24,16},{32,24},{40,32},{48,40},{56,48},{1,57}... | collective-permute-start | bytes 98312 | tf_op jit(solution)/shard_map/ppermute | solution.py:19
  18.6 4.4 %copy-start.15 = (bf16[1024,8]{0,1:T(8,128)(2,1)S(1)}, bf16[1024,8]{0,1:T(8,128)(2,1)}, u32[]{:S(2)}) copy-start(bf16[1024,8]{0,1:T(8,128)(2,1)} %param.13) | copy-start | bytes 49156
  19.5 6.6 %collective-permute-start.1 = (bf16[128,1,8,128]{0,3,2,1:T(8,128)(2,1)S(1)}, bf16[128,1,8,128]{0,3,2,1:T(8,128)(2,1)S(1)}, u32[]{:S(2)}, u32[]{:S(2)}) collective-permute-start(bf16[128,1,8,128]{0,3,2,1:T(8,128)(2,1)S(1)} %get-tuple-element.15), channel_id=1, source_target_pairs={{0,56},{8,0},{16,8},{24,16},{32,24},{40,32},{48,40},{56,48},{1,57}... | collective-permute-start | bytes 786440 | tf_op jit(solution)/shard_map/ppermute | solution.py:19
  20.6 5.5 %copy-start.1 = (bf16[1,256,1,8,128]{1,4,3,2,0:T(8,128)(2,1)}, bf16[1,256,1,8,128]{1,4,3,2,0:T(8,128)(2,1)S(1)}, u32[]{:S(2)}) copy-start(bf16[1,256,1,8,128]{1,4,3,2,0:T(8,128)(2,1)S(1)} %copy.17) | copy-start | bytes 1572868
  21.6 10.2 %collective-permute-start.3 = (bf16[128,1,8,128]{0,3,2,1:T(8,128)(2,1)}, bf16[128,1,8,128]{0,3,2,1:T(8,128)(2,1)}, u32[]{:S(2)}, u32[]{:S(2)}) collective-permute-start(bf16[128,1,8,128]{0,3,2,1:T(8,128)(2,1)} %get-tuple-element.21), channel_id=1, source_target_pairs={{0,56},{8,0},{16,8},{24,16},{32,24},{40,32},{48,40},{56,48},{1,57}... | collective-permute-start | bytes 786440 | tf_op jit(solution)/shard_map/ppermute | solution.py:19
  24.1 2.0 copy-start.11
  28.7 3.1 copy-start.2
  28.7 3.1 copy-start.5
  28.9 4.3 %copy-start.10 = (bf16[1,256,1,128]{3,1,2,0:T(8,128)(2,1)S(1)}, bf16[1,256,1,128]{3,1,2,0:T(8,128)(2,1)}, u32[]{:S(2)}) copy-start(bf16[1,256,1,128]{3,1,2,0:T(8,128)(2,1)} %param.10) | copy-start | bytes 196612
  29.0 4.3 %copy-start.14 = (bf16[128,128]{1,0:T(8,128)(2,1)S(1)}, bf16[128,128]{1,0:T(8,128)(2,1)}, u32[]{:S(2)}) copy-start(bf16[128,128]{1,0:T(8,128)(2,1)} %get-tuple-element.30) | copy-start | bytes 98308
  33.2 5.2 %copy-start.7 = (bf16[256,128]{1,0:T(8,128)(2,1)}, bf16[256,128]{1,0:T(8,128)(2,1)S(1)}, u32[]{:S(2)}) copy-start(bf16[256,128]{1,0:T(8,128)(2,1)S(1)} %fusion.9) | copy-start | bytes 196612
  33.2 1.5 copy-start.4
  33.2 1.5 copy-start.13
  34.7 1.6 copy-start.18
  36.3 1.3 copy-start.6
  36.8 4.1 %collective-permute-start.5 = (bf16[128,1,128]{2,0,1:T(8,128)(2,1)S(1)}, bf16[128,1,128]{2,0,1:T(8,128)(2,1)S(1)}, u32[]{:S(2)}, u32[]{:S(2)}) collective-permute-start(bf16[128,1,128]{2,0,1:T(8,128)(2,1)S(1)} %get-tuple-element.24), channel_id=1, source_target_pairs={{0,8},{8,16},{16,24},{24,32},{32,40},{40,48},{48,56},{56,0},{1,9},... | collective-permute-start | bytes 98312 | tf_op jit(solution)/shard_map/ppermute | solution.py:19
  37.6 7.9 %copy-start.16 = (bf16[8,1,8,128]{3,2,1,0:T(8,128)(2,1)S(1)}, bf16[8,1,8,128]{3,2,1,0:T(8,128)(2,1)}, u32[]{:S(2)}) copy-start(bf16[8,1,8,128]{3,2,1,0:T(8,128)(2,1)} %param.14) | copy-start | bytes 49156
  38.1 7.3 %collective-permute-start.4 = (bf16[128,1,8,128]{0,3,2,1:T(8,128)(2,1)S(1)}, bf16[128,1,8,128]{0,3,2,1:T(8,128)(2,1)S(1)}, u32[]{:S(2)}, u32[]{:S(2)}) collective-permute-start(bf16[128,1,8,128]{0,3,2,1:T(8,128)(2,1)S(1)} %get-tuple-element.17), channel_id=1, source_target_pairs={{0,8},{8,16},{16,24},{24,32},{32,40},{40,48},{48,56},{56,0},{1,9},... | collective-permute-start | bytes 786440 | tf_op jit(solution)/shard_map/ppermute | solution.py:19
  38.4 49.1 %copy-start.8 = (bf16[256,128]{1,0:T(8,128)(2,1)S(1)}, bf16[256,128]{1,0:T(8,128)(2,1)}, u32[]{:S(2)}) copy-start(bf16[256,128]{1,0:T(8,128)(2,1)} %copy-done.7) | copy-start | bytes 196612
  38.4 49.1 %collective-permute-start.6 = (bf16[128,1,128]{2,0,1:T(8,128)(2,1)S(1)}, bf16[128,1,128]{2,0,1:T(8,128)(2,1)S(1)}, u32[]{:S(2)}, u32[]{:S(2)}) collective-permute-start(bf16[128,1,128]{2,0,1:T(8,128)(2,1)S(1)} %get-tuple-element.22), channel_id=1, source_target_pairs={{0,8},{8,16},{16,24},{24,32},{32,40},{40,48},{48,56},{56,0},{1,9},... | collective-permute-start | bytes 98312 | tf_op jit(solution)/shard_map/ppermute | solution.py:19
  (3 other events, 3.3 us)
Sparse Core Ops, SparseCore 0:
  87.6 211.9 all-reduce.3
where the time goes:
time: 310 us; the launch traced here: 309 us
  waiting for transfers between devices  221 us (71%)
  blocking collectives  39.9 us (13%)
  between operations  15 us (5%)
  local copies, waits for them, and re-layouts  11.9 us (4%)
  starting transfers between devices  9.82 us (3%)
  matrix products  8.73 us (3%)
    psum x1, waiting for transfers between devices, on_device(): lax.psum((down_product, up_product), ('dp', 'ctx'))  210 us
    psum x1, blocking collectives, on_device(): rank_total, grad_total = lax.psum((low_rank_product, grad_part), 'head')  39.9 us
    ppermute x7, waiting for transfers between devices, shifted_2(): return lax.ppermute(value, axis, pairs)  11.1 us
    ppermute x7, starting transfers between devices, shifted_2(): return lax.ppermute(value, axis, pairs)  9.78 us
    unnamed x43, local copies, waits for them, and re-layouts  6.26 us
  transfers between devices with their start and end apart: 8, of which 5 were waited for; matrix products, arithmetic and copies ran while one was open for 5% of the time, Pallas kernels for 0%

commit v1 on v0

v1 whole, which is shorter than its diff:
```python
import functools
import math

import jax
import jax.numpy as jnp
from jax import lax
from jax.experimental import pallas as pl
from jax.experimental.pallas import tpu as pltpu
from jax.sharding import PartitionSpec as P

ADAPTER_SCALE = 2.0
BLOCKED = -1e30
MESH = pl.DeviceIdType.MESH
F32 = jnp.float32
BF16 = jnp.bfloat16
NT = (((1,), (1,)), ((), ()))
NN = (((1,), (0,)), ((), ()))
TN = (((0,), (0,)), ((), ()))


def mm(a, b, dims):
    return lax.dot_general(a, b, dims, preferred_element_type=F32)


def kernel(
    dims,
    q_in, k_in, v_in, do_in, x_in, at_in, u_in, len_in,
    dq_out, dk_out, dv_out, down_out, up_out,
    q_s, do_s, x_s, at_s, u_s, k_s, v_s,
    dq32, dq16, dqcat, dkv_out,
    acc_ke, acc_ve, acc_kl, acc_vl, ret_send, ret_recv,
    ri_buf, rg_buf, up_part, up_recv, up_all, dn_part, dn_recv, dn_all,
    load_sem, out_sem, kv_send, kv_recv, ret_sems, ri_sems, rg_sems,
    up_sems, upg_sems, dn_sems, dng_sems,
):
    nd, nc, nh, half, group, rank = dims
    rows = 2 * half
    hq = half * group
    here_d, here_c, here_h = lax.axis_index("dp"), lax.axis_index("ctx"), lax.axis_index("head")
    shifted = jnp.where(here_h < nh // 2, 1, 0)
    is_shifted = here_h < nh // 2
    early = shifted * half
    late = (1 - shifted) * half
    early_q = pl.multiple_of(shifted * hq, hq)
    late_q = pl.multiple_of((1 - shifted) * hq, hq)
    early_m = pl.multiple_of(early, half)
    late_m = pl.multiple_of(late, half)
    group_count = nd * nc
    me = here_d * nc + here_c
    after_c = lax.rem(here_c + 1, nc)
    before_c = lax.rem(here_c + nc - 1, nc)

    def local(src, dst, sem):
        return pltpu.make_async_copy(src, dst, sem)

    loads = [
        local(x_in, x_s, load_sem.at[0]),
        local(at_in, at_s, load_sem.at[1]),
        local(k_in.at[pl.ds(early_m, half)], k_s.at[pl.ds(0, half)], load_sem.at[2]),
        local(v_in.at[pl.ds(early_m, half)], v_s.at[pl.ds(0, half)], load_sem.at[3]),
        local(q_in.at[pl.ds(early_q, hq)], q_s.at[pl.ds(0, hq)], load_sem.at[4]),
        local(do_in.at[pl.ds(early_q, hq)], do_s.at[pl.ds(0, hq)], load_sem.at[5]),
        local(k_in.at[pl.ds(late_m, half)], k_s.at[pl.ds(rows, half)], load_sem.at[6]),
        local(v_in.at[pl.ds(late_m, half)], v_s.at[pl.ds(rows, half)], load_sem.at[7]),
        local(q_in.at[pl.ds(late_q, hq)], q_s.at[pl.ds(hq, hq)], load_sem.at[8]),
        local(do_in.at[pl.ds(late_q, hq)], do_s.at[pl.ds(hq, hq)], load_sem.at[9]),
        local(u_in, u_s, load_sem.at[10]),
    ]
    for load in loads:
        load.start()

    barrier = pltpu.get_barrier_semaphore()

    def greet_group(step, carry):
        peer = lax.rem(me + step, group_count)
        pl.semaphore_signal(
            barrier, inc=1, device_id=(peer // nc, lax.rem(peer, nc), here_h), device_id_type=MESH
        )
        return carry

    def greet_head(step, carry):
        pl.semaphore_signal(
            barrier, inc=1, device_id=(here_d, here_c, lax.rem(here_h + step, nh)), device_id_type=MESH
        )
        return carry

    lax.fori_loop(1, group_count, greet_group, 0)
    lax.fori_loop(1, nh, greet_head, 0)

    loads[0].wait()
    loads[1].wait()
    ri_buf[here_h] = mm(at_s[...], x_s[...], NT)

    pl.semaphore_wait(barrier, group_count - 1 + nh - 1)
    loads[2].wait()
    loads[3].wait()

    def kv_copy(ref, at):
        return pltpu.make_async_remote_copy(
            src_ref=ref.at[pl.ds(0, half)],
            dst_ref=ref.at[pl.ds(half, half)],
            send_sem=kv_send.at[at],
            recv_sem=kv_recv.at[at],
            device_id=(here_d, after_c, here_h),
            device_id_type=MESH,
        )

    @pl.when(is_shifted)
    def _():
        kv_copy(k_s, 0).start()
        kv_copy(v_s, 1).start()

    @pl.when(jnp.logical_not(is_shifted))
    def _():
        k_s[half:rows] = k_s[0:half]
        v_s[half:rows] = v_s[0:half]

    def head_exchange(buf, sems):
        def send(step, carry):
            peer = lax.rem(here_h + step, nh)
            pltpu.make_async_remote_copy(
                src_ref=buf.at[here_h],
                dst_ref=buf.at[here_h],
                send_sem=sems.at[0],
                recv_sem=sems.at[1],
                device_id=(here_d, here_c, peer),
                device_id_type=MESH,
            ).start()
            return carry

        lax.fori_loop(1, nh, send, 0)

    def many(buf, count, sem):
        part = buf.at[pl.ds(0, count)]
        return pltpu.make_async_copy(part, part, sem)

    head_exchange(ri_buf, ri_sems)

    length = len_in[0]
    softmax_scale = 1.0 / math.sqrt(128)
    exp_scale = softmax_scale * math.log2(math.e)
    chunk = 256
    per = chunk // group
    start_early = here_c * rows + early
    start_late = here_c * rows + late
    start_prev = jnp.where(is_shifted, before_c * rows + half, start_early)

    def attend(at, has_prev, base, accum_k, accum_v):
        keys_from = half if has_prev else 0
        count = rows if has_prev else half
        row0 = (hq if has_prev else 0) + at * chunk
        queries = q_s[row0 : row0 + chunk]
        live = do_s[row0 : row0 + chunk]
        keys = k_s[keys_from : keys_from + count]
        values = v_s[keys_from : keys_from + count]
        scores = mm(keys, queries, NT)
        prob_grad = mm(values, live, NT)
        key_at = lax.broadcasted_iota(jnp.int32, (half, chunk), 0)
        query_at = lax.broadcasted_iota(jnp.int32, (half, chunk), 1) // group + at * per
        allowed = (key_at <= query_at) & ((key_at < length - base) | (key_at == query_at))
        if has_prev:
            allowed = jnp.concatenate([key_at < length - start_prev, allowed], axis=0)
        scores = jnp.where(allowed, scores, BLOCKED)
        top = jnp.max(scores, axis=0, keepdims=True)
        weights = jnp.exp2((scores - top) * exp_scale)
        total = jnp.sum(weights, axis=0, keepdims=True)
        query_row = lax.broadcasted_iota(jnp.int32, (1, chunk), 1) // group + at * per
        inverse = jnp.where(query_row < length - base, 1.0 / total, 0.0)
        probs = weights * inverse
        probs_low = probs.astype(BF16)
        out_dot = jnp.sum(probs_low.astype(F32) * prob_grad, axis=0, keepdims=True)
        score_grad = (probs * (prob_grad - out_dot)).astype(BF16)
        query_grad = mm(score_grad, keys, TN) * softmax_scale
        to = pl.ds(pl.multiple_of((late_q if has_prev else early_q) + at * chunk, chunk), chunk)
        dq32[to, :] = query_grad
        dq16[to, :] = query_grad.astype(BF16)
        part_k = mm(score_grad, queries, NN)
        part_v = mm(probs_low, live, NN)
        if at == 0:
            accum_k[...] = part_k
            accum_v[...] = part_v
        else:
            accum_k[...] += part_k
            accum_v[...] += part_v

    loads[4].wait()
    loads[5].wait()
    for at in range(hq // chunk):
        attend(at, False, start_early, acc_ke, acc_ve)

    for at in (6, 7, 8, 9):
        loads[at].wait()

    @pl.when(is_shifted)
    def _():
        kv_copy(k_s, 0).wait()
        kv_copy(v_s, 1).wait()

    for at in range(hq // chunk):
        attend(at, True, start_late, acc_kl, acc_vl)

    dq_copy = local(dq16, dq_out, out_sem.at[0])
    dq_copy.start()

    ret_copy = pltpu.make_async_remote_copy(
        src_ref=ret_send,
        dst_ref=ret_recv,
        send_sem=ret_sems.at[0],
        recv_sem=ret_sems.at[1],
        device_id=(here_d, before_c, here_h),
        device_id_type=MESH,
    )

    for g in range(group):
        dqcat[:, g * 128 : (g + 1) * 128] = dq32[pl.ds(g, rows, stride=group), :].astype(BF16)
    loads[10].wait()
    up_flat = jnp.concatenate(
        [u_s[...].astype(F32).reshape(rank, group, 128)[:, g, :] for g in range(group)], axis=1
    ).astype(BF16)
    rg_buf[here_h] = mm(up_flat, dqcat[...], NT)
    head_exchange(rg_buf, rg_sems)

    @pl.when(is_shifted)
    def _():
        ret_send[0:half] = acc_kl[0:half].astype(BF16)
        ret_send[half:rows] = acc_vl[0:half].astype(BF16)
        ret_copy.start()

    def scatter(part, recv, sems):
        recv[me] = part[here_c]

        def send(step, carry):
            peer = lax.rem(me + step, group_count)
            peer_c = lax.rem(peer, nc)
            pltpu.make_async_remote_copy(
                src_ref=part.at[peer_c],
                dst_ref=recv.at[me],
                send_sem=sems.at[0],
                recv_sem=sems.at[1],
                device_id=(peer // nc, peer_c, here_h),
                device_id_type=MESH,
            ).start()
            return carry

        lax.fori_loop(1, group_count, send, 0)

    def gather(recv, whole, scatter_sems, sems):
        many(recv, group_count - 1, scatter_sems.at[1]).wait()
        whole[here_c] = jnp.sum(recv[...], axis=0)

        def send(step, carry):
            pltpu.make_async_remote_copy(
                src_ref=whole.at[here_c],
                dst_ref=whole.at[here_c],
                send_sem=sems.at[0],
                recv_sem=sems.at[1],
                device_id=(here_d, lax.rem(here_c + step, nc), here_h),
                device_id_type=MESH,
            ).start()
            return carry

        lax.fori_loop(1, nc, send, 0)

    many(ri_buf, nh - 1, ri_sems.at[1]).wait()
    rank_input = jnp.sum(ri_buf[...], axis=0).astype(BF16)
    up_grad = mm(rank_input, dqcat[...], NN) * ADAPTER_SCALE
    for t in range(nc):
        up_part[t] = up_grad[:, t * 128 : (t + 1) * 128]
    scatter(up_part, up_recv, up_sems)

    many(rg_buf, nh - 1, rg_sems.at[1]).wait()
    rank_grad = jnp.sum(rg_buf[...], axis=0).astype(BF16)
    down_grad = mm(rank_grad, x_s[...], NN) * ADAPTER_SCALE
    for t in range(nc):
        dn_part[t] = down_grad[:, t * 128 : (t + 1) * 128]
    scatter(dn_part, dn_recv, dn_sems)

    gather(up_recv, up_all, up_sems, upg_sems)
    gather(dn_recv, dn_all, dn_sems, dng_sems)

    dkv_out[0, pl.ds(late_m, half), :] = (acc_kl[half:rows] * softmax_scale).astype(BF16)
    dkv_out[1, pl.ds(late_m, half), :] = acc_vl[half:rows].astype(BF16)

    @pl.when(is_shifted)
    def _():
        ret_copy.wait()
        dkv_out[0, pl.ds(early_m, half), :] = (
            (acc_ke[...] + ret_recv[0:half].astype(F32)) * softmax_scale
        ).astype(BF16)
        dkv_out[1, pl.ds(early_m, half), :] = (acc_ve[...] + ret_recv[half:rows].astype(F32)).astype(BF16)

    @pl.when(jnp.logical_not(is_shifted))
    def _():
        dkv_out[0, pl.ds(early_m, half), :] = ((acc_ke[...] + acc_kl[0:half]) * softmax_scale).astype(BF16)
        dkv_out[1, pl.ds(early_m, half), :] = (acc_ve[...] + acc_vl[0:half]).astype(BF16)

    dk_copy = local(dkv_out.at[0], dk_out, out_sem.at[1])
    dv_copy = local(dkv_out.at[1], dv_out, out_sem.at[2])
    dk_copy.start()
    dv_copy.start()

    many(up_all, nc - 1, upg_sems.at[1]).wait()
    up_whole = up_all[...]
    for r in range(rank):
        up_out[r] = up_whole[:, r, :]
    many(dn_all, nc - 1, dng_sems.at[1]).wait()
    for t in range(nc):
        down_out[:, t * 128 : (t + 1) * 128] = dn_all[t]

    many(ri_buf, nh - 1, ri_sems.at[0]).wait()
    many(rg_buf, nh - 1, rg_sems.at[0]).wait()
    many(up_recv, group_count - 1, up_sems.at[0]).wait()
    many(dn_recv, group_count - 1, dn_sems.at[0]).wait()
    many(up_all, nc - 1, upg_sems.at[0]).wait()
    many(dn_all, nc - 1, dng_sems.at[0]).wait()
    dq_copy.wait()
    dk_copy.wait()
    dv_copy.wait()


def on_device(sizes, q, k, v, do, x, adapter_down, adapter_up, lengths):
    nd, nc, nh = sizes
    rows, group, width = q.shape[1], q.shape[3], q.shape[4]
    rank, model = adapter_down.shape[1], x.shape[2]
    half = rows // 2
    dims = (nd, nc, nh, half, group, rank)
    hbm = pl.BlockSpec(memory_space=pl.ANY)
    vmem = pl.BlockSpec(memory_space=pltpu.VMEM)
    smem = pl.BlockSpec(memory_space=pltpu.SMEM)
    pair = pltpu.SemaphoreType.DMA((2,))
    tiles = (nc, rank, 128)
    all_tiles = (nd * nc, rank, 128)
    outs = pl.pallas_call(
        functools.partial(kernel, dims),
        out_shape=(
            jax.ShapeDtypeStruct((rows * group, width), BF16),
            jax.ShapeDtypeStruct((rows, width), BF16),
            jax.ShapeDtypeStruct((rows, width), BF16),
            jax.ShapeDtypeStruct((rank, model), F32),
            jax.ShapeDtypeStruct((rank, group, width), F32),
        ),
        in_specs=[hbm] * 7 + [smem],
        out_specs=(hbm, hbm, hbm, vmem, vmem),
        scratch_shapes=[
            pltpu.VMEM((rows * group, width), BF16),
            pltpu.VMEM((rows * group, width), BF16),
            pltpu.VMEM((rows, model), BF16),
            pltpu.VMEM((rank, model), BF16),
            pltpu.VMEM((rank * group, width), BF16),
            pltpu.VMEM((rows + half, width), BF16),
            pltpu.VMEM((rows + half, width), BF16),
            pltpu.VMEM((rows * group, width), F32),
            pltpu.VMEM((rows * group, width), BF16),
            pltpu.VMEM((rows, group * width), BF16),
            pltpu.VMEM((2, rows, width), BF16),
            pltpu.VMEM((half, width), F32),
            pltpu.VMEM((half, width), F32),
            pltpu.VMEM((rows, width), F32),
            pltpu.VMEM((rows, width), F32),
            pltpu.VMEM((rows, width), BF16),
            pltpu.VMEM((rows, width), BF16),
            pltpu.VMEM((nh, rank, rows), F32),
            pltpu.VMEM((nh, rank, rows), F32),
            pltpu.VMEM(tiles, F32),
            pltpu.VMEM(all_tiles, F32),
            pltpu.VMEM(tiles, F32),
            pltpu.VMEM(tiles, F32),
            pltpu.VMEM(all_tiles, F32),
            pltpu.VMEM(tiles, F32),
            pltpu.SemaphoreType.DMA((11,)),
            pltpu.SemaphoreType.DMA((3,)),
            pair, pair, pair, pair, pair, pair, pair, pair, pair,
        ],
        compiler_params=pltpu.CompilerParams(
            collective_id=0, has_side_effects=True, vmem_limit_bytes=40 * 1024 * 1024
        ),
        name="attention_and_rank_gradients",
    )(
        q.reshape(rows * group, width),
        k.reshape(rows, width),
        v.reshape(rows, width),
        do.reshape(rows * group, width),
        x.reshape(rows, model),
        adapter_down.T,
        adapter_up.reshape(rank * group, width),
        lengths,
    )
    dq, dk, dv, down, up = outs
    return (
        dq.reshape(q.shape),
        dk.reshape(k.shape),
        dv.reshape(v.shape),
        down.T,
        up.reshape(adapter_up.shape),
    )


def solution(mesh):
    sizes = (mesh.shape["dp"], mesh.shape["ctx"], mesh.shape["head"])
    return jax.shard_map(
        functools.partial(on_device, sizes),
        mesh=mesh,
        in_specs=(
            P("dp", "ctx", "head", None, None),
            P("dp", "ctx", "head", None),
            P("dp", "ctx", "head", None),
            P("dp", "ctx", "head", None, None),
            P("dp", "ctx", "head"),
            P("head", None),
            P(None, "head", None, None),
            P("dp"),
        ),
        out_specs=(
            P("dp", "ctx", "head", None, None),
            P("dp", "ctx", "head", None),
            P("dp", "ctx", "head", None),
            P("head", None),
            P(None, "head", None, None),
        ),
        check_vma=False,
    )
```

time: 310 us -> 42.8 us (0.14)
  waiting for transfers between devices: 221 us -> 0 us
  blocking collectives: 39.9 us -> 0 us
  Pallas kernels: 0 us -> 31.5 us
  between operations: 15 us -> 1.31 us
  starting transfers between devices: 9.82 us -> 0 us
  matrix products: 8.73 us -> 0 us
    psum x1 -> x0, waiting for transfers between devices: 210 us -> none  [on_device(): lax.psum((down_product, up_product), ('dp', 'ctx'))]
    psum x1 -> x0, blocking collectives: 39.9 us -> none  [on_device(): rank_total, grad_total = lax.psum((low_rank_product, grad_part), 'head')]
    pallas_call x0 -> x1, Pallas kernels: none -> 31.5 us  [on_device(): pl.pallas_call(functools.partial(kernel, dims), out_shape=(jax.ShapeDtype...]
    ppermute x7 -> x0, waiting for transfers between devices: 11.1 us -> none  [shifted_2(): return lax.ppermute(value, axis, pairs)]
    ppermute x7 -> x0, starting transfers between devices: 9.78 us -> none  [shifted_2(): return lax.ppermute(value, axis, pairs)]
    dot_general x9 -> x0, matrix products: 6.79 us -> none  [the longest x1 1.5 us: attend_rows(): jnp.einsum('igd,jd->gij', grad_block, values_head, preferred_element_type...]
    unnamed x43 -> x19, local copies, waits for them, and re-layouts: 6.26 us -> 9.51 us
  transfers between devices with their start and end apart: 8 -> 0, of which waited for: 5 -> 0; matrix products, arithmetic and copies ran while one was open for 5% -> 0% of each run, Pallas kernels for 0% -> 0%
where the time goes in v1:
time: 42.8 us; the launch traced here: 42.3 us
  Pallas kernels  31.5 us (74%)
  local copies, waits for them, and re-layouts  9.51 us (22%)
  between operations  1.31 us (3%)
    pallas_call x1, Pallas kernels, on_device(): pl.pallas_call(functools.partial(kernel, dims), out_shape=(jax.ShapeDtype...  31.5 us
    unnamed x19, local copies, waits for them, and re-layouts  9.51 us

profile of v1, /device:TPU:1, one launch (start us, length us, event | category | flops | bytes accessed | tf_op | source)
XLA Modules:
  0.0 42.3 jit_solution(7054587449271178121)
XLA Ops:
  1.3 0.0 copy-start
  1.3 1.0 %copy-done = bf16[1,256,1,8,128]{4,3,2,1,0:T(8,128)(2,1)S(1)} copy-done((bf16[1,256,1,8,128]{4,3,2,1,0:T(8,128)(2,1)S(1)}, bf16[1,256,1,8,128]{4,3,2,1,0:T(8,128)(2,1)}, u32[]{:S(2)}) %copy-start) | copy-done | bytes 524312
  2.3 0.0 copy-start.1
  2.3 1.0 %copy-done.1 = bf16[1,256,1,8,128]{4,3,2,1,0:T(8,128)(2,1)S(1)} copy-done((bf16[1,256,1,8,128]{4,3,2,1,0:T(8,128)(2,1)S(1)}, bf16[1,256,1,8,128]{4,3,2,1,0:T(8,128)(2,1)}, u32[]{:S(2)}) %copy-start.1) | copy-done | bytes 524312
  3.4 0.0 copy-start.2
  3.4 1.0 %copy-done.2 = bf16[1,256,1024]{2,1,0:T(8,128)(2,1)S(1)} copy-done((bf16[1,256,1024]{2,1,0:T(8,128)(2,1)S(1)}, bf16[1,256,1024]{2,1,0:T(8,128)(2,1)}, u32[]{:S(2)}) %copy-start.2) | copy-done | bytes 524312
  4.4 0.0 copy-start.3
  4.4 0.8 %copy-done.3 = bf16[1,256,1,128]{3,1,2,0:T(8,128)(2,1)S(1)} copy-done((bf16[1,256,1,128]{3,1,2,0:T(8,128)(2,1)S(1)}, bf16[1,256,1,128]{3,1,2,0:T(8,128)(2,1)}, u32[]{:S(2)}) %copy-start.3) | copy-done | bytes 65560
  5.2 0.0 copy-start.4
  5.2 0.8 %copy-done.4 = bf16[1,256,1,128]{3,1,2,0:T(8,128)(2,1)S(1)} copy-done((bf16[1,256,1,128]{3,1,2,0:T(8,128)(2,1)S(1)}, bf16[1,256,1,128]{3,1,2,0:T(8,128)(2,1)}, u32[]{:S(2)}) %copy-start.4) | copy-done | bytes 65560
  6.1 0.0 copy-start.5
  6.1 0.7 %copy-done.5 = bf16[1024,8]{0,1:T(8,128)(2,1)S(1)} copy-done((bf16[1024,8]{0,1:T(8,128)(2,1)S(1)}, bf16[1024,8]{0,1:T(8,128)(2,1)}, u32[]{:S(2)}) %copy-start.5) | copy-done | bytes 16408
  6.8 0.0 copy-start.6
  6.8 0.7 %copy-done.6 = bf16[8,1,8,128]{3,2,1,0:T(8,128)(2,1)S(1)} copy-done((bf16[8,1,8,128]{3,2,1,0:T(8,128)(2,1)S(1)}, bf16[8,1,8,128]{3,2,1,0:T(8,128)(2,1)}, u32[]{:S(2)}) %copy-start.6) | copy-done | bytes 16408
  7.5 31.5 %attention_and_rank_gradients.1 = (bf16[2048,128]{1,0:T(8,128)(2,1)S(1)}, bf16[256,128]{1,0:T(8,128)(2,1)S(1)}, bf16[256,128]{1,0:T(8,128)(2,1)S(1)}, f32[8,1024]{1,0:T(8,128)S(1)}, f32[8,8,128]{2,1,0:T(8,128)S(1)}) custom-call(bf16[2048,128]{1,0:T(8,128)(2,1)S(1)} %bitcast.16, bf16[256,128]{1,0:T(8,128)(2,1)S(1)} %bitcast.20, ...), custom_call_target="tpu_custom_call" | custom-call | tf_op jit(solution)/shard_map/attention_and_rank_gradients/pallas_call | solution.py:333
  39.1 0.8 %copy.21 = bf16[1,256,1,8,128]{4,3,2,1,0:T(8,128)(2,1)} copy(bf16[1,256,1,8,128]{4,3,2,1,0:T(8,128)(2,1)S(1)} %bitcast.19) | data formatting | bytes 1048576
  39.9 0.6 %copy.22 = bf16[1,256,1,128]{3,1,2,0:T(8,128)(2,1)} copy(bf16[1,256,1,128]{3,1,2,0:T(8,128)(2,1)S(1)} %bitcast.23) | data formatting | bytes 131072
  40.5 0.6 %copy.23 = bf16[1,256,1,128]{3,1,2,0:T(8,128)(2,1)} copy(bf16[1,256,1,128]{3,1,2,0:T(8,128)(2,1)S(1)} %bitcast.22) | data formatting | bytes 131072
  41.1 0.6 %copy.24 = f32[1024,8]{0,1:T(8,128)} copy(f32[1024,8]{0,1:T(8,128)S(1)} %bitcast.25) | data formatting | bytes 65536
  41.7 0.6 %copy.25 = f32[8,1,8,128]{3,2,1,0:T(8,128)} copy(f32[8,1,8,128]{3,2,1,0:T(8,128)S(1)} %bitcast.24) | data formatting | bytes 65536
Async XLA Ops:
  1.3 1.0 %copy-start = (bf16[1,256,1,8,128]{4,3,2,1,0:T(8,128)(2,1)S(1)}, bf16[1,256,1,8,128]{4,3,2,1,0:T(8,128)(2,1)}, u32[]{:S(2)}) copy-start(bf16[1,256,1,8,128]{4,3,2,1,0:T(8,128)(2,1)} %param.8) | copy-start | bytes 1572868
  2.3 1.0 %copy-start.1 = (bf16[1,256,1,8,128]{4,3,2,1,0:T(8,128)(2,1)S(1)}, bf16[1,256,1,8,128]{4,3,2,1,0:T(8,128)(2,1)}, u32[]{:S(2)}) copy-start(bf16[1,256,1,8,128]{4,3,2,1,0:T(8,128)(2,1)} %param.11) | copy-start | bytes 1572868
  3.4 1.0 %copy-start.2 = (bf16[1,256,1024]{2,1,0:T(8,128)(2,1)S(1)}, bf16[1,256,1024]{2,1,0:T(8,128)(2,1)}, u32[]{:S(2)}) copy-start(bf16[1,256,1024]{2,1,0:T(8,128)(2,1)} %param.12) | copy-start | bytes 1572868
  4.4 0.8 %copy-start.3 = (bf16[1,256,1,128]{3,1,2,0:T(8,128)(2,1)S(1)}, bf16[1,256,1,128]{3,1,2,0:T(8,128)(2,1)}, u32[]{:S(2)}) copy-start(bf16[1,256,1,128]{3,1,2,0:T(8,128)(2,1)} %param.9) | copy-start | bytes 196612
  5.2 0.8 %copy-start.4 = (bf16[1,256,1,128]{3,1,2,0:T(8,128)(2,1)S(1)}, bf16[1,256,1,128]{3,1,2,0:T(8,128)(2,1)}, u32[]{:S(2)}) copy-start(bf16[1,256,1,128]{3,1,2,0:T(8,128)(2,1)} %param.10) | copy-start | bytes 196612
  6.1 0.7 %copy-start.5 = (bf16[1024,8]{0,1:T(8,128)(2,1)S(1)}, bf16[1024,8]{0,1:T(8,128)(2,1)}, u32[]{:S(2)}) copy-start(bf16[1024,8]{0,1:T(8,128)(2,1)} %param.13) | copy-start | bytes 49156
  6.8 0.7 %copy-start.6 = (bf16[8,1,8,128]{3,2,1,0:T(8,128)(2,1)S(1)}, bf16[8,1,8,128]{3,2,1,0:T(8,128)(2,1)}, u32[]{:S(2)}) copy-start(bf16[8,1,8,128]{3,2,1,0:T(8,128)(2,1)} %param.14) | copy-start | bytes 49156

commit v2 on v1

v2 whole, which is shorter than its diff:
```python
import functools
import math

import jax
import jax.numpy as jnp
from jax import lax
from jax.experimental import pallas as pl
from jax.experimental.pallas import tpu as pltpu
from jax.sharding import PartitionSpec as P

ADAPTER_SCALE = 2.0
BLOCKED = -1e30
MESH = pl.DeviceIdType.MESH
F32 = jnp.float32
BF16 = jnp.bfloat16
NT = (((1,), (1,)), ((), ()))
NN = (((1,), (0,)), ((), ()))
TN = (((0,), (0,)), ((), ()))


def mm(a, b, dims):
    return lax.dot_general(a, b, dims, preferred_element_type=F32)


def kernel(
    dims,
    q_in, k_in, v_in, do_in, x_in, at_in, u_in, len_in,
    dq_out, dkv_out, down_out, up_out,
    q_s, do_s, x_s, at_s, u_s, k_s, v_s,
    dq32, dqcat, own_scores, own_grads,
    acc_ke, acc_ve, acc_kl, acc_vl, ret_send, ret_recv,
    ri_buf, rg_buf, up_a, up_ar, up_b, up_c, dn_a, dn_ar, dn_b, dn_c,
    load_sem, kv_send, kv_recv, ret_sems, ri_sems, rg_sems,
    up_asem, up_bsem, up_csem, dn_asem, dn_bsem, dn_csem,
):
    nd, nc, nh, half, group, rank = dims
    rows = 2 * half
    hq = half * group
    here_d, here_c, here_h = lax.axis_index("dp"), lax.axis_index("ctx"), lax.axis_index("head")
    core = lax.rem(here_d, 2)
    is_shifted = here_h < nh // 2
    shifted = jnp.where(is_shifted, 1, 0)
    early = shifted * half
    late = (1 - shifted) * half
    early_q = pl.multiple_of(shifted * hq, hq)
    late_q = pl.multiple_of((1 - shifted) * hq, hq)
    early_m = pl.multiple_of(early, half)
    late_m = pl.multiple_of(late, half)
    after_c = lax.rem(here_c + 1, nc)
    before_c = lax.rem(here_c + nc - 1, nc)

    def in_head(step):
        return (here_d, here_c, lax.rem(here_h + step, nh))

    def in_ctx(step):
        return (here_d, lax.rem(here_c + step, nc), here_h)

    def in_dp(step):
        return (lax.rem(here_d + step, nd), here_c, here_h)

    barrier = pltpu.get_barrier_semaphore()
    for peers, count in ((in_ctx, nc), (in_head, nh), (in_dp, nd)):
        for step in range(1, count):
            pl.semaphore_signal(barrier, inc=1, device_id=peers(step), device_id_type=MESH)

    def local(src, dst, at):
        copy = pltpu.make_async_copy(src, dst, load_sem.at[at])
        copy.start()
        return copy

    load_ke = local(k_in.at[pl.ds(early_m, half)], k_s.at[pl.ds(0, half)], 0)
    load_ve = local(v_in.at[pl.ds(early_m, half)], v_s.at[pl.ds(0, half)], 1)
    load_qe = local(q_in.at[pl.ds(early_q, hq)], q_s.at[pl.ds(0, hq)], 2)
    load_de = local(do_in.at[pl.ds(early_q, hq)], do_s.at[pl.ds(0, hq)], 3)
    load_x = local(x_in, x_s, 5)
    load_at = local(at_in, at_s, 6)
    load_kl = local(k_in.at[pl.ds(late_m, half)], k_s.at[pl.ds(rows, half)], 7)
    load_vl = local(v_in.at[pl.ds(late_m, half)], v_s.at[pl.ds(rows, half)], 8)
    load_ql = local(q_in.at[pl.ds(late_q, hq)], q_s.at[pl.ds(hq, hq)], 9)
    load_dl = local(do_in.at[pl.ds(late_q, hq)], do_s.at[pl.ds(hq, hq)], 10)
    load_u = local(u_in, u_s, 11)

    def remote(src, dst, sends, recvs, peer):
        return pltpu.make_async_remote_copy(
            src_ref=src, dst_ref=dst, send_sem=sends, recv_sem=recvs, device_id=peer, device_id_type=MESH
        )

    def many(buf, count, sem):
        part = buf.at[pl.ds(0, count)]
        return pltpu.make_async_copy(part, part, sem)

    softmax_scale = 1.0 / math.sqrt(128)
    exp_scale = softmax_scale * math.log2(math.e)
    chunk = 256
    per = chunk // group
    chunks = hq // chunk
    start_early = here_c * rows + early
    start_late = here_c * rows + late
    start_prev = jnp.where(is_shifted, before_c * rows + half, start_early)
    load_ke.wait()
    load_ve.wait()
    length = len_in[0]

    def own_part(at, keys, values, queries, live, base):
        key_at = lax.broadcasted_iota(jnp.int32, (half, chunk), 0)
        query_at = lax.broadcasted_iota(jnp.int32, (half, chunk), 1) // group + at * per
        allowed = (key_at <= query_at) & ((key_at < length - base) | (key_at == query_at))
        scores = jnp.where(allowed, mm(keys, queries, NT), BLOCKED)
        return scores, mm(values, live, NT)

    def finish(at, scores, prob_grad, keys, queries, live, base, to, accum_k, accum_v):
        top = jnp.max(scores, axis=0, keepdims=True)
        weights = jnp.exp2((scores - top) * exp_scale)
        total = jnp.sum(weights, axis=0, keepdims=True)
        query_row = lax.broadcasted_iota(jnp.int32, (1, chunk), 1) // group + at * per
        inverse = jnp.where(query_row < length - base, 1.0 / total, 0.0)
        probs = weights * inverse
        probs_low = probs.astype(BF16)
        out_dot = jnp.sum(probs_low.astype(F32) * prob_grad, axis=0, keepdims=True)
        score_grad = (probs * (prob_grad - out_dot)).astype(BF16)
        query_grad = mm(score_grad, keys, TN) * softmax_scale
        place = pl.ds(pl.multiple_of(to + at * chunk, chunk), chunk)
        dq32[place, :] = query_grad
        dq_out[place, :] = query_grad.astype(BF16)
        part_k = mm(score_grad, queries, NN)
        part_v = mm(probs_low, live, NN)
        if at == 0:
            accum_k[...] = part_k
            accum_v[...] = part_v
        else:
            accum_k[...] += part_k
            accum_v[...] += part_v

    load_qe.wait()
    load_de.wait()
    for at in range(chunks):
        queries = q_s[at * chunk : (at + 1) * chunk]
        live = do_s[at * chunk : (at + 1) * chunk]
        keys = k_s[0:half]
        scores, prob_grad = own_part(at, keys, v_s[0:half], queries, live, start_early)
        finish(at, scores, prob_grad, keys, queries, live, start_early, early_q, acc_ke, acc_ve)

    pl.semaphore_wait(barrier, nc + nh + nd - 3)

    kv_copies = [
        remote(ref.at[pl.ds(0, half)], ref.at[pl.ds(half, half)], kv_send.at[at], kv_recv.at[at], in_ctx(1))
        for at, ref in enumerate((k_s, v_s))
    ]

    @pl.when(is_shifted)
    def _():
        for copy in kv_copies:
            copy.start()

    @pl.when(jnp.logical_not(is_shifted))
    def _():
        k_s[half:rows] = k_s[0:half]
        v_s[half:rows] = v_s[0:half]

    def head_exchange(buf, sems):
        for step in range(1, nh):
            remote(buf.at[here_h], buf.at[here_h], sems.at[0], sems.at[1], in_head(step)).start()

    load_x.wait()
    load_at.wait()
    ri_buf[here_h] = mm(at_s[...], x_s[...], NT)
    head_exchange(ri_buf, ri_sems)

    load_kl.wait()
    load_vl.wait()
    load_ql.wait()
    load_dl.wait()
    for at in range(chunks):
        place = slice(hq + at * chunk, hq + (at + 1) * chunk)
        scores, prob_grad = own_part(
            at, k_s[rows : rows + half], v_s[rows : rows + half], q_s[place], do_s[place], start_late
        )
        own_scores[at] = scores
        own_grads[at] = prob_grad
    load_u.wait()
    up_flat = jnp.concatenate(
        [u_s[...].astype(F32).reshape(rank, group, 128)[:, g, :] for g in range(group)], axis=1
    ).astype(BF16)

    @pl.when(is_shifted)
    def _():
        for copy in kv_copies:
            copy.wait()

    prev_seen = lax.broadcasted_iota(jnp.int32, (half, chunk), 0) < length - start_prev
    for at in range(chunks):
        queries = q_s[hq + at * chunk : hq + (at + 1) * chunk]
        live = do_s[hq + at * chunk : hq + (at + 1) * chunk]
        prev_scores = jnp.where(prev_seen, mm(k_s[half:rows], queries, NT), BLOCKED)
        scores = jnp.concatenate([prev_scores, own_scores[at]], axis=0)
        prob_grad = jnp.concatenate([mm(v_s[half:rows], live, NT), own_grads[at]], axis=0)
        finish(
            at, scores, prob_grad, k_s[half : rows + half], queries, live, start_late, late_q, acc_kl, acc_vl
        )

    for g in range(group):
        dqcat[:, g * 128 : (g + 1) * 128] = dq32[pl.ds(g, rows, stride=group), :].astype(BF16)
    rg_buf[here_h] = mm(up_flat, dqcat[...], NT)
    head_exchange(rg_buf, rg_sems)

    ret_copy = remote(ret_send, ret_recv, ret_sems.at[0], ret_sems.at[1], in_ctx(nc - 1))

    @pl.when(is_shifted)
    def _():
        ret_send[0:half] = acc_kl[0:half].astype(BF16)
        ret_send[half:rows] = acc_vl[0:half].astype(BF16)
        ret_copy.start()

    quarter = group * 128 // 4

    def send_halves(total, part, recv, sems):
        for side in range(2):
            at = 2 * side * quarter
            part[side] = jnp.concatenate(
                [total[:, at : at + quarter], total[:, at + quarter : at + 2 * quarter]], axis=0
            ).astype(BF16)
        recv[here_d] = part[core]
        for step in range(1, nd):
            peer = in_dp(step)
            remote(part.at[lax.rem(peer[0], 2)], recv.at[here_d], sems.at[0], sems.at[1], peer).start()

    def send_over_ctx(recv, sems, onward, onward_sems):
        many(recv, nd - 1, sems.at[1]).wait()
        onward[here_c] = jnp.sum(recv[...].astype(F32), axis=0).astype(BF16)
        for step in range(1, nc):
            remote(
                onward.at[here_c], onward.at[here_c], onward_sems.at[0], onward_sems.at[1], in_ctx(step)
            ).start()

    def send_to_core(recv, sems, onward, onward_sems):
        many(recv, nc - 1, sems.at[1]).wait()
        onward[core] = jnp.sum(recv[...].astype(F32), axis=0)
        peer = (here_d + 1 - 2 * core, here_c, here_h)
        copy = remote(onward.at[core], onward.at[core], onward_sems.at[0], onward_sems.at[1], peer)
        copy.start()
        return copy

    many(ri_buf, nh - 1, ri_sems.at[1]).wait()
    rank_input = jnp.sum(ri_buf[...], axis=0).astype(BF16)
    send_halves(mm(rank_input, dqcat[...], NN) * ADAPTER_SCALE, up_a, up_ar, up_asem)

    dkv_out[0, pl.ds(late_m, half), :] = (acc_kl[half:rows] * softmax_scale).astype(BF16)
    dkv_out[1, pl.ds(late_m, half), :] = acc_vl[half:rows].astype(BF16)
    send_over_ctx(up_ar, up_asem, up_b, up_bsem)

    many(rg_buf, nh - 1, rg_sems.at[1]).wait()
    rank_grad = jnp.sum(rg_buf[...], axis=0).astype(BF16)
    send_halves(mm(rank_grad, x_s[...], NN) * ADAPTER_SCALE, dn_a, dn_ar, dn_asem)

    @pl.when(is_shifted)
    def _():
        ret_copy.wait()
        dkv_out[0, pl.ds(early_m, half), :] = (
            (acc_ke[...] + ret_recv[0:half].astype(F32)) * softmax_scale
        ).astype(BF16)
        dkv_out[1, pl.ds(early_m, half), :] = (acc_ve[...] + ret_recv[half:rows].astype(F32)).astype(BF16)

    @pl.when(jnp.logical_not(is_shifted))
    def _():
        dkv_out[0, pl.ds(early_m, half), :] = ((acc_ke[...] + acc_kl[0:half]) * softmax_scale).astype(BF16)
        dkv_out[1, pl.ds(early_m, half), :] = (acc_ve[...] + acc_vl[0:half]).astype(BF16)

    send_over_ctx(dn_ar, dn_asem, dn_b, dn_bsem)
    up_core = send_to_core(up_b, up_bsem, up_c, up_csem)
    dn_core = send_to_core(dn_b, dn_bsem, dn_c, dn_csem)

    def whole(ref):
        return jnp.concatenate(
            [ref[side, rank * row : rank * (row + 1)] for side in range(2) for row in range(2)], axis=1
        )

    up_core.wait()
    up_whole = whole(up_c)
    for g in range(group):
        up_out[:, g, :] = up_whole[:, g * 128 : (g + 1) * 128]
    for buf, count, sem in (
        (ri_buf, nh - 1, ri_sems), (rg_buf, nh - 1, rg_sems), (up_ar, nd - 1, up_asem),
        (dn_ar, nd - 1, dn_asem), (up_b, nc - 1, up_bsem), (dn_b, nc - 1, dn_bsem),
    ):
        many(buf, count, sem.at[0]).wait()
    dn_core.wait()
    down_out[...] = whole(dn_c)


def write_out(*refs):
    dq, dkv, down, up, dq_out, dk_out, dv_out, down_out, up_out, sems = refs
    pairs = ((dq, dq_out), (dkv.at[0], dk_out), (dkv.at[1], dv_out), (down, down_out), (up, up_out))
    copies = [pltpu.make_async_copy(src, dst, sems.at[at]) for at, (src, dst) in enumerate(pairs)]
    for copy in copies:
        copy.start()
    for copy in copies:
        copy.wait()


def on_device(sizes, q, k, v, do, x, adapter_down, adapter_up, lengths):
    nd, nc, nh = sizes
    rows, group, width = q.shape[1], q.shape[3], q.shape[4]
    rank, model = adapter_down.shape[1], x.shape[2]
    half = rows // 2
    hq = half * group
    dims = (nd, nc, nh, half, group, rank)
    hbm = pl.BlockSpec(memory_space=pltpu.HBM)
    anywhere = pl.BlockSpec(memory_space=pl.ANY)
    vmem = pl.BlockSpec(memory_space=pltpu.VMEM)
    pair = pltpu.SemaphoreType.DMA((2,))
    packed = (2 * rank, group * width // 4)
    results = (
        ((rows * group, width), BF16),
        ((2, rows, width), BF16),
        ((rank, model), F32),
        ((rank, group, width), F32),
    )
    operands = (
        q.reshape(rows * group, width),
        k.reshape(rows, width),
        v.reshape(rows, width),
        do.reshape(rows * group, width),
        x.reshape(rows, model),
        adapter_down.T,
        adapter_up.reshape(rank * group, width),
    )
    made = pl.pallas_call(
        functools.partial(kernel, dims),
        out_shape=tuple(pltpu.VMEM(*one) for one in results),
        in_specs=[hbm] * 7 + [pl.BlockSpec(memory_space=pltpu.SMEM)],
        out_specs=(vmem,) * 4,
        scratch_shapes=[
            pltpu.VMEM((rows * group, width), BF16),
            pltpu.VMEM((rows * group, width), BF16),
            pltpu.VMEM((rows, model), BF16),
            pltpu.VMEM((rank, model), BF16),
            pltpu.VMEM((rank * group, width), BF16),
            pltpu.VMEM((rows + half, width), BF16),
            pltpu.VMEM((rows + half, width), BF16),
            pltpu.VMEM((rows * group, width), F32),
            pltpu.VMEM((rows, group * width), BF16),
            pltpu.VMEM((hq // 256, half, 256), F32),
            pltpu.VMEM((hq // 256, half, 256), F32),
            pltpu.VMEM((half, width), F32),
            pltpu.VMEM((half, width), F32),
            pltpu.VMEM((rows, width), F32),
            pltpu.VMEM((rows, width), F32),
            pltpu.VMEM((rows, width), BF16),
            pltpu.VMEM((rows, width), BF16),
            pltpu.VMEM((nh, rank, rows), F32),
            pltpu.VMEM((nh, rank, rows), F32),
        ]
        + [
            pltpu.VMEM((2,) + packed, BF16),
            pltpu.VMEM((nd,) + packed, BF16),
            pltpu.VMEM((nc,) + packed, BF16),
            pltpu.VMEM((2,) + packed, F32),
        ]
        * 2
        + [pltpu.SemaphoreType.DMA((12,))]
        + [pair] * 11,
        compiler_params=pltpu.CompilerParams(
            collective_id=0, has_side_effects=True, vmem_limit_bytes=40 * 1024 * 1024
        ),
        name="attention_and_rank_gradients",
    )(*(pltpu.with_memory_space_constraint(one, pltpu.HBM) for one in operands), lengths)
    dq, dk, dv, down, up = pl.pallas_call(
        write_out,
        out_shape=(
            jax.ShapeDtypeStruct(*results[0]),
            jax.ShapeDtypeStruct((rows, width), BF16),
            jax.ShapeDtypeStruct((rows, width), BF16),
            jax.ShapeDtypeStruct(*results[2]),
            jax.ShapeDtypeStruct(*results[3]),
        ),
        in_specs=[anywhere] * 4,
        out_specs=(hbm,) * 5,
        scratch_shapes=[pltpu.SemaphoreType.DMA((5,))],
        name="write_results",
    )(*made)
    return (
        dq.reshape(q.shape),
        dk.reshape(k.shape),
        dv.reshape(v.shape),
        down.T,
        up.reshape(adapter_up.shape),
    )


def solution(mesh):
    sizes = (mesh.shape["dp"], mesh.shape["ctx"], mesh.shape["head"])
    return jax.shard_map(
        functools.partial(on_device, sizes),
        mesh=mesh,
        in_specs=(
            P("dp", "ctx", "head", None, None),
            P("dp", "ctx", "head", None),
            P("dp", "ctx", "head", None),
            P("dp", "ctx", "head", None, None),
            P("dp", "ctx", "head"),
            P("head", None),
            P(None, "head", None, None),
            P("dp"),
        ),
        out_specs=(
            P("dp", "ctx", "head", None, None),
            P("dp", "ctx", "head", None),
            P("dp", "ctx", "head", None),
            P("head", None),
            P(None, "head", None, None),
        ),
        check_vma=False,
    )
```

time: 42.8 us -> 56.2 us (1.31)
  Pallas kernels: 31.5 us -> 52.2 us
  local copies, waits for them, and re-layouts: 9.51 us -> 2.62 us
    pallas_call x1 -> x2, Pallas kernels: 31.5 us -> 52.2 us  [the longest x1 29.2 us: on_device(): pl.pallas_call(functools.partial(kernel, dims), out_shape=tuple((pltpu.VM...]
    unnamed x19 -> x8, local copies, waits for them, and re-layouts: 9.51 us -> 2.62 us
where the time goes in v2:
time: 56.2 us; the launch traced here: 56.1 us
  Pallas kernels  52.2 us (93%)
  local copies, waits for them, and re-layouts  2.62 us (5%)
  between operations  1.3 us (2%)
    pallas_call x1, Pallas kernels, on_device(): pl.pallas_call(functools.partial(kernel, dims), out_shape=tuple((pltpu.VM...  29.2 us
    pallas_call x1, Pallas kernels, on_device(): pl.pallas_call(write_out, out_shape=(jax.ShapeDtypeStruct(*results[0]), j...  23 us
    unnamed x8, local copies, waits for them, and re-layouts  2.62 us

profile of v2, /device:TPU:1, one launch (start us, length us, event | category | flops | bytes accessed | tf_op | source)
XLA Modules:
  0.0 56.1 jit_solution(8849034565694940282)
XLA Ops:
  1.3 29.2 %attention_and_rank_gradients.1 = (bf16[2048,128]{1,0:T(8,128)(2,1)S(1)}, bf16[2,256,128]{2,1,0:T(8,128)(2,1)S(1)}, f32[8,1024]{1,0:T(8,128)S(1)}, f32[8,8,128]{2,1,0:T(8,128)S(1)}) custom-call(bf16[2048,128]{1,0:T(8,128)(2,1)} %bitcast.16, bf16[256,128]{1,0:T(8,128)(2,1)} %bitcast.19, bf16[256,128]{1,0:T(8,128)(2,1)} %bitcast.20, ...), custom_call_target="tpu_custom_call" | custom-call | tf_op jit(solution)/shard_map/attention_and_rank_gradients/pallas_call | solution.py:327
  30.5 0.0 copy-start
  30.5 0.8 %copy-done = bf16[2048,128]{1,0:T(8,128)(2,1)} copy-done((bf16[2048,128]{1,0:T(8,128)(2,1)}, bf16[2048,128]{1,0:T(8,128)(2,1)S(1)}, u32[]{:S(2)}) %copy-start) | copy-done | bytes 524312
  31.2 0.0 copy-start.1
  31.2 0.6 %copy-done.1 = bf16[2,256,128]{2,1,0:T(8,128)(2,1)} copy-done((bf16[2,256,128]{2,1,0:T(8,128)(2,1)}, bf16[2,256,128]{2,1,0:T(8,128)(2,1)S(1)}, u32[]{:S(2)}) %copy-start.1) | copy-done | bytes 131096
  31.9 0.0 copy-start.2
  31.9 0.6 %copy-done.2 = f32[8,1024]{1,0:T(8,128)} copy-done((f32[8,1024]{1,0:T(8,128)}, f32[8,1024]{1,0:T(8,128)S(1)}, u32[]{:S(2)}) %copy-start.2) | copy-done | bytes 32792
  32.5 0.0 copy-start.3
  32.5 0.6 %copy-done.3 = f32[8,8,128]{2,1,0:T(8,128)} copy-done((f32[8,8,128]{2,1,0:T(8,128)}, f32[8,8,128]{2,1,0:T(8,128)S(1)}, u32[]{:S(2)}) %copy-start.3) | copy-done | bytes 32792
  33.1 23.0 %write_results.1 = (bf16[2048,128]{1,0:T(8,128)(2,1)}, bf16[256,128]{1,0:T(8,128)(2,1)}, bf16[256,128]{1,0:T(8,128)(2,1)}, f32[8,1024]{1,0:T(8,128)}, f32[8,8,128]{2,1,0:T(8,128)}) custom-call(bf16[2048,128]{1,0:T(8,128)(2,1)} %copy-done, bf16[2,256,128]{2,1,0:T(8,128)(2,1)} %copy-done.1, f32[8,1024]{1,0:T(8,128)} %copy-done.2, f32[8,8,128]{2,1,0:T(8,128)} %copy-done.3), custom_call_target="tpu_custom_call" | custom-call | tf_op jit(solution)/shard_map/write_results/pallas_call | solution.py:367
Async XLA Ops:
  30.5 0.8 %copy-start = (bf16[2048,128]{1,0:T(8,128)(2,1)}, bf16[2048,128]{1,0:T(8,128)(2,1)S(1)}, u32[]{:S(2)}) copy-start(bf16[2048,128]{1,0:T(8,128)(2,1)S(1)} %get-tuple-element.14.refs_0_) | copy-start | bytes 1572868
  31.2 0.6 %copy-start.1 = (bf16[2,256,128]{2,1,0:T(8,128)(2,1)}, bf16[2,256,128]{2,1,0:T(8,128)(2,1)S(1)}, u32[]{:S(2)}) copy-start(bf16[2,256,128]{2,1,0:T(8,128)(2,1)S(1)} %get-tuple-element.15.refs_1_) | copy-start | bytes 393220
  31.9 0.6 %copy-start.2 = (f32[8,1024]{1,0:T(8,128)}, f32[8,1024]{1,0:T(8,128)S(1)}, u32[]{:S(2)}) copy-start(f32[8,1024]{1,0:T(8,128)S(1)} %get-tuple-element.16.refs_2_) | copy-start | bytes 98308
  32.5 0.6 %copy-start.3 = (f32[8,8,128]{2,1,0:T(8,128)}, f32[8,8,128]{2,1,0:T(8,128)S(1)}, u32[]{:S(2)}) copy-start(f32[8,8,128]{2,1,0:T(8,128)S(1)} %get-tuple-element.17.refs_3_) | copy-start | bytes 98308

commit v3 on v2

--- a/solution.py
+++ b/solution.py
@@ -305,7 +305,6 @@
     hq = half * group
     dims = (nd, nc, nh, half, group, rank)
     hbm = pl.BlockSpec(memory_space=pltpu.HBM)
-    anywhere = pl.BlockSpec(memory_space=pl.ANY)
     vmem = pl.BlockSpec(memory_space=pltpu.VMEM)
     pair = pltpu.SemaphoreType.DMA((2,))
     packed = (2 * rank, group * width // 4)
@@ -373,11 +372,11 @@
             jax.ShapeDtypeStruct(*results[2]),
             jax.ShapeDtypeStruct(*results[3]),
         ),
-        in_specs=[anywhere] * 4,
+        in_specs=[vmem] * 4,
         out_specs=(hbm,) * 5,
         scratch_shapes=[pltpu.SemaphoreType.DMA((5,))],
         name="write_results",
-    )(*made)
+    )(*(pltpu.with_memory_space_constraint(one, pltpu.VMEM) for one in made))
     return (
         dq.reshape(q.shape),
         dk.reshape(k.shape),

time: 56.2 us -> 31.5 us (0.56)
  Pallas kernels: 52.2 us -> 30.1 us
  local copies, waits for them, and re-layouts: 2.62 us -> 0 us
    pallas_call x1, Pallas kernels: 23 us -> 0.89 us  [on_device(): pl.pallas_call(write_out, out_shape=(jax.ShapeDtypeStruct(*results[0]), j...]
    unnamed x8 -> x0, local copies, waits for them, and re-layouts: 2.62 us -> none
where the time goes in v3:
time: 31.5 us; the launch traced here: 31.3 us
  Pallas kernels  30.1 us (96%)
  between operations  1.29 us (4%)
    pallas_call x1, Pallas kernels, on_device(): pl.pallas_call(functools.partial(kernel, dims), out_shape=tuple((pltpu.VM...  29.2 us
    pallas_call x1, Pallas kernels, on_device(): pl.pallas_call(write_out, out_shape=(jax.ShapeDtypeStruct(*results[0]), j...  0.89 us

profile of v3, /device:TPU:1, one launch (start us, length us, event | category | flops | bytes accessed | tf_op | source)
XLA Modules:
  0.0 31.3 jit_solution(10369580828478688888)
XLA Ops:
  1.3 29.2 %attention_and_rank_gradients.1 = (bf16[2048,128]{1,0:T(8,128)(2,1)S(1)}, bf16[2,256,128]{2,1,0:T(8,128)(2,1)S(1)}, f32[8,1024]{1,0:T(8,128)S(1)}, f32[8,8,128]{2,1,0:T(8,128)S(1)}) custom-call(bf16[2048,128]{1,0:T(8,128)(2,1)} %bitcast.16, bf16[256,128]{1,0:T(8,128)(2,1)} %bitcast.19, bf16[256,128]{1,0:T(8,128)(2,1)} %bitcast.20, ...), custom_call_target="tpu_custom_call" | custom-call | tf_op jit(solution)/shard_map/attention_and_rank_gradients/pallas_call | solution.py:326
  30.5 0.9 %write_results.1 = (bf16[2048,128]{1,0:T(8,128)(2,1)}, bf16[256,128]{1,0:T(8,128)(2,1)}, bf16[256,128]{1,0:T(8,128)(2,1)}, f32[8,1024]{1,0:T(8,128)}, f32[8,8,128]{2,1,0:T(8,128)}) custom-call(bf16[2048,128]{1,0:T(8,128)(2,1)S(1)} %get-tuple-element.14.refs_0_, bf16[2,256,128]{2,1,0:T(8,128)(2,1)S(1)} %get-tuple-element.15.refs_1_, ...), custom_call_target="tpu_custom_call" | custom-call | tf_op jit(solution)/shard_map/write_results/pallas_call | solution.py:366

commit v4 on v3

--- a/solution.py
+++ b/solution.py
@@ -10,12 +10,17 @@
 
 ADAPTER_SCALE = 2.0
 BLOCKED = -1e30
+CHUNK = 256
 MESH = pl.DeviceIdType.MESH
 F32 = jnp.float32
 BF16 = jnp.bfloat16
 NT = (((1,), (1,)), ((), ()))
 NN = (((1,), (0,)), ((), ()))
 TN = (((0,), (0,)), ((), ()))
+
+
+def far_first(count):
+    return sorted(range(1, count), key=lambda step: -min(step, count - step))
 
 
 def mm(a, b, dims):
@@ -29,15 +34,14 @@
     q_s, do_s, x_s, at_s, u_s, k_s, v_s,
     dq32, dqcat, own_scores, own_grads,
     acc_ke, acc_ve, acc_kl, acc_vl, ret_send, ret_recv,
-    ri_buf, rg_buf, up_a, up_ar, up_b, up_c, dn_a, dn_ar, dn_b, dn_c,
+    ri_buf, rg_buf, up_a, up_b, dn_a, dn_b,
     load_sem, kv_send, kv_recv, ret_sems, ri_sems, rg_sems,
-    up_asem, up_bsem, up_csem, dn_asem, dn_bsem, dn_csem,
+    up_asem, up_bsem, dn_asem, dn_bsem,
 ):
     nd, nc, nh, half, group, rank = dims
     rows = 2 * half
     hq = half * group
     here_d, here_c, here_h = lax.axis_index("dp"), lax.axis_index("ctx"), lax.axis_index("head")
-    core = lax.rem(here_d, 2)
     is_shifted = here_h < nh // 2
     shifted = jnp.where(is_shifted, 1, 0)
     early = shifted * half
@@ -60,7 +64,7 @@
 
     barrier = pltpu.get_barrier_semaphore()
     for peers, count in ((in_ctx, nc), (in_head, nh), (in_dp, nd)):
-        for step in range(1, count):
+        for step in far_first(count):
             pl.semaphore_signal(barrier, inc=1, device_id=peers(step), device_id_type=MESH)
 
     def local(src, dst, at):
@@ -91,7 +95,7 @@
 
     softmax_scale = 1.0 / math.sqrt(128)
     exp_scale = softmax_scale * math.log2(math.e)
-    chunk = 256
+    chunk = CHUNK
     per = chunk // group
     chunks = hq // chunk
     start_early = here_c * rows + early
@@ -99,7 +103,7 @@
     start_prev = jnp.where(is_shifted, before_c * rows + half, start_early)
     load_ke.wait()
     load_ve.wait()
-    length = len_in[0]
+    length = len_in[...]
 
     def own_part(at, keys, values, queries, live, base):
         key_at = lax.broadcasted_iota(jnp.int32, (half, chunk), 0)
@@ -158,7 +162,7 @@
         v_s[half:rows] = v_s[0:half]
 
     def head_exchange(buf, sems):
-        for step in range(1, nh):
+        for step in far_first(nh):
             remote(buf.at[here_h], buf.at[here_h], sems.at[0], sems.at[1], in_head(step)).start()
 
     load_x.wait()
@@ -211,46 +215,37 @@
         ret_send[half:rows] = acc_vl[0:half].astype(BF16)
         ret_copy.start()
 
-    quarter = group * 128 // 4
-
-    def send_halves(total, part, recv, sems):
-        for side in range(2):
-            at = 2 * side * quarter
-            part[side] = jnp.concatenate(
-                [total[:, at : at + quarter], total[:, at + quarter : at + 2 * quarter]], axis=0
-            ).astype(BF16)
-        recv[here_d] = part[core]
-        for step in range(1, nd):
-            peer = in_dp(step)
-            remote(part.at[lax.rem(peer[0], 2)], recv.at[here_d], sems.at[0], sems.at[1], peer).start()
+    wide = group * 128 // 2
+
+    def send_over_dp(total, recv, sems):
+        recv[here_d] = jnp.concatenate([total[:, :wide], total[:, wide:]], axis=0).astype(BF16)
+        for step in range(nd - 1, 0, -1):
+            remote(recv.at[here_d], recv.at[here_d], sems.at[0], sems.at[1], in_dp(step)).start()
 
     def send_over_ctx(recv, sems, onward, onward_sems):
         many(recv, nd - 1, sems.at[1]).wait()
         onward[here_c] = jnp.sum(recv[...].astype(F32), axis=0).astype(BF16)
-        for step in range(1, nc):
+        for step in far_first(nc):
             remote(
                 onward.at[here_c], onward.at[here_c], onward_sems.at[0], onward_sems.at[1], in_ctx(step)
             ).start()
 
-    def send_to_core(recv, sems, onward, onward_sems):
+    def whole(recv, sems):
         many(recv, nc - 1, sems.at[1]).wait()
-        onward[core] = jnp.sum(recv[...].astype(F32), axis=0)
-        peer = (here_d + 1 - 2 * core, here_c, here_h)
-        copy = remote(onward.at[core], onward.at[core], onward_sems.at[0], onward_sems.at[1], peer)
-        copy.start()
-        return copy
+        total = jnp.sum(recv[...].astype(F32), axis=0)
+        return jnp.concatenate([total[:rank], total[rank:]], axis=1)
 
     many(ri_buf, nh - 1, ri_sems.at[1]).wait()
     rank_input = jnp.sum(ri_buf[...], axis=0).astype(BF16)
-    send_halves(mm(rank_input, dqcat[...], NN) * ADAPTER_SCALE, up_a, up_ar, up_asem)
+    send_over_dp(mm(rank_input, dqcat[...], NN) * ADAPTER_SCALE, up_a, up_asem)
 
     dkv_out[0, pl.ds(late_m, half), :] = (acc_kl[half:rows] * softmax_scale).astype(BF16)
     dkv_out[1, pl.ds(late_m, half), :] = acc_vl[half:rows].astype(BF16)
-    send_over_ctx(up_ar, up_asem, up_b, up_bsem)
+    send_over_ctx(up_a, up_asem, up_b, up_bsem)
 
     many(rg_buf, nh - 1, rg_sems.at[1]).wait()
     rank_grad = jnp.sum(rg_buf[...], axis=0).astype(BF16)
-    send_halves(mm(rank_grad, x_s[...], NN) * ADAPTER_SCALE, dn_a, dn_ar, dn_asem)
+    send_over_dp(mm(rank_grad, x_s[...], NN) * ADAPTER_SCALE, dn_a, dn_asem)
 
     @pl.when(is_shifted)
     def _():
@@ -265,26 +260,16 @@
         dkv_out[0, pl.ds(early_m, half), :] = ((acc_ke[...] + acc_kl[0:half]) * softmax_scale).astype(BF16)
         dkv_out[1, pl.ds(early_m, half), :] = (acc_ve[...] + acc_vl[0:half]).astype(BF16)
 
-    send_over_ctx(dn_ar, dn_asem, dn_b, dn_bsem)
-    up_core = send_to_core(up_b, up_bsem, up_c, up_csem)
-    dn_core = send_to_core(dn_b, dn_bsem, dn_c, dn_csem)
-
-    def whole(ref):
-        return jnp.concatenate(
-            [ref[side, rank * row : rank * (row + 1)] for side in range(2) for row in range(2)], axis=1
-        )
-
-    up_core.wait()
-    up_whole = whole(up_c)
+    send_over_ctx(dn_a, dn_asem, dn_b, dn_bsem)
+    up_whole = whole(up_b, up_bsem)
     for g in range(group):
         up_out[:, g, :] = up_whole[:, g * 128 : (g + 1) * 128]
     for buf, count, sem in (
-        (ri_buf, nh - 1, ri_sems), (rg_buf, nh - 1, rg_sems), (up_ar, nd - 1, up_asem),
-        (dn_ar, nd - 1, dn_asem), (up_b, nc - 1, up_bsem), (dn_b, nc - 1, dn_bsem),
+        (ri_buf, nh - 1, ri_sems), (rg_buf, nh - 1, rg_sems), (up_a, nd - 1, up_asem),
+        (dn_a, nd - 1, dn_asem), (up_b, nc - 1, up_bsem), (dn_b, nc - 1, dn_bsem),
     ):
         many(buf, count, sem.at[0]).wait()
-    dn_core.wait()
-    down_out[...] = whole(dn_c)
+    down_out[...] = whole(dn_b, dn_bsem)
 
 
 def write_out(*refs):
@@ -307,7 +292,7 @@
     hbm = pl.BlockSpec(memory_space=pltpu.HBM)
     vmem = pl.BlockSpec(memory_space=pltpu.VMEM)
     pair = pltpu.SemaphoreType.DMA((2,))
-    packed = (2 * rank, group * width // 4)
+    packed = (2 * rank, group * width // 2)
     results = (
         ((rows * group, width), BF16),
         ((2, rows, width), BF16),
@@ -326,7 +311,7 @@
     made = pl.pallas_call(
         functools.partial(kernel, dims),
         out_shape=tuple(pltpu.VMEM(*one) for one in results),
-        in_specs=[hbm] * 7 + [pl.BlockSpec(memory_space=pltpu.SMEM)],
+        in_specs=[hbm] * 7 + [vmem],
         out_specs=(vmem,) * 4,
         scratch_shapes=[
             pltpu.VMEM((rows * group, width), BF16),
@@ -338,8 +323,8 @@
             pltpu.VMEM((rows + half, width), BF16),
             pltpu.VMEM((rows * group, width), F32),
             pltpu.VMEM((rows, group * width), BF16),
-            pltpu.VMEM((hq // 256, half, 256), F32),
-            pltpu.VMEM((hq // 256, half, 256), F32),
+            pltpu.VMEM((hq // CHUNK, half, CHUNK), F32),
+            pltpu.VMEM((hq // CHUNK, half, CHUNK), F32),
             pltpu.VMEM((half, width), F32),
             pltpu.VMEM((half, width), F32),
             pltpu.VMEM((rows, width), F32),
@@ -350,19 +335,20 @@
             pltpu.VMEM((nh, rank, rows), F32),
         ]
         + [
-            pltpu.VMEM((2,) + packed, BF16),
             pltpu.VMEM((nd,) + packed, BF16),
             pltpu.VMEM((nc,) + packed, BF16),
-            pltpu.VMEM((2,) + packed, F32),
         ]
         * 2
         + [pltpu.SemaphoreType.DMA((12,))]
-        + [pair] * 11,
+        + [pair] * 9,
         compiler_params=pltpu.CompilerParams(
             collective_id=0, has_side_effects=True, vmem_limit_bytes=40 * 1024 * 1024
         ),
         name="attention_and_rank_gradients",
-    )(*(pltpu.with_memory_space_constraint(one, pltpu.HBM) for one in operands), lengths)
+    )(
+        *(pltpu.with_memory_space_constraint(one, pltpu.HBM) for one in operands),
+        pltpu.with_memory_space_constraint(jnp.broadcast_to(lengths[:, None], (1, CHUNK)), pltpu.VMEM),
+    )
     dq, dk, dv, down, up = pl.pallas_call(
         write_out,
         out_shape=(

time: 31.5 us -> 29.7 us (0.943)
  Pallas kernels: 30.1 us -> 28 us
    pallas_call x1, Pallas kernels: 29.2 us -> 27.1 us  [on_device(): pl.pallas_call(functools.partial(kernel, dims), out_shape=tuple((pltpu.VM...]
where the time goes in v4:
time: 29.7 us; the launch traced here: 29.3 us
  Pallas kernels  28 us (94%)
  between operations  1.29 us (4%)
    pallas_call x1, Pallas kernels, on_device(): pl.pallas_call(functools.partial(kernel, dims), out_shape=tuple((pltpu.VM...  27.1 us
    pallas_call x1, Pallas kernels, on_device(): pl.pallas_call(write_out, out_shape=(jax.ShapeDtypeStruct(*results[0]), j...  0.89 us

profile of v4, /device:TPU:1, one launch (start us, length us, event | category | flops | bytes accessed | tf_op | source)
XLA Modules:
  0.0 29.3 jit_solution(14432263560391222944)
XLA Ops:
  1.3 27.1 %attention_and_rank_gradients.1 = (bf16[2048,128]{1,0:T(8,128)(2,1)S(1)}, bf16[2,256,128]{2,1,0:T(8,128)(2,1)S(1)}, f32[8,1024]{1,0:T(8,128)S(1)}, f32[8,8,128]{2,1,0:T(8,128)S(1)}) custom-call(bf16[2048,128]{1,0:T(8,128)(2,1)} %bitcast.18, bf16[256,128]{1,0:T(8,128)(2,1)} %bitcast.21, bf16[256,128]{1,0:T(8,128)(2,1)} %bitcast.22, ...), custom_call_target="tpu_custom_call" | custom-call | tf_op jit(solution)/shard_map/attention_and_rank_gradients/pallas_call | solution.py:311
  28.4 0.9 %write_results.1 = (bf16[2048,128]{1,0:T(8,128)(2,1)}, bf16[256,128]{1,0:T(8,128)(2,1)}, bf16[256,128]{1,0:T(8,128)(2,1)}, f32[8,1024]{1,0:T(8,128)}, f32[8,8,128]{2,1,0:T(8,128)}) custom-call(bf16[2048,128]{1,0:T(8,128)(2,1)S(1)} %get-tuple-element.14.refs_0_, bf16[2,256,128]{2,1,0:T(8,128)(2,1)S(1)} %get-tuple-element.15.refs_1_, ...), custom_call_target="tpu_custom_call" | custom-call | tf_op jit(solution)/shard_map/write_results/pallas_call | solution.py:352
  (1 shorter events, 0.0 us)

commit v5 on v4

--- a/solution.py
+++ b/solution.py
@@ -32,11 +32,11 @@
     q_in, k_in, v_in, do_in, x_in, at_in, u_in, len_in,
     dq_out, dkv_out, down_out, up_out,
     q_s, do_s, x_s, at_s, u_s, k_s, v_s,
-    dq32, dqcat, own_scores, own_grads,
+    dq32, dqcat, own_scores, own_grads, sg_e, pr_e, sg_l, pr_l,
     acc_ke, acc_ve, acc_kl, acc_vl, ret_send, ret_recv,
     ri_buf, rg_buf, up_a, up_b, dn_a, dn_b,
     load_sem, kv_send, kv_recv, ret_sems, ri_sems, rg_sems,
-    up_asem, up_bsem, dn_asem, dn_bsem,
+    up_asem, up_bsem, dn_asem, dn_bsem, relay_sems,
 ):
     nd, nc, nh, half, group, rank = dims
     rows = 2 * half
@@ -62,10 +62,22 @@
     def in_dp(step):
         return (lax.rem(here_d + step, nd), here_c, here_h)
 
+    flip = (here_d, here_c, here_h + 1 - 2 * lax.rem(here_h, 2))
+    beside = [in_ctx(step) for step in sorted({1, nc - 1})]
+    two_off = [in_ctx(step) for step in sorted({2, nc - 2}) if 0 < step < nc]
+    near = (
+        [flip]
+        + [in_head(step) for step in sorted({2, 4, nh - 2}) if 0 < step < nh]
+        + [in_dp(step) for step in range(nd - 1, 0, -1)]
+        + beside
+    )
+
+    def tell(semaphore, peers):
+        for peer in peers:
+            pl.semaphore_signal(semaphore, inc=1, device_id=peer, device_id_type=MESH)
+
     barrier = pltpu.get_barrier_semaphore()
-    for peers, count in ((in_ctx, nc), (in_head, nh), (in_dp, nd)):
-        for step in far_first(count):
-            pl.semaphore_signal(barrier, inc=1, device_id=peers(step), device_id_type=MESH)
+    tell(barrier, near)
 
     def local(src, dst, at):
         copy = pltpu.make_async_copy(src, dst, load_sem.at[at])
@@ -112,7 +124,7 @@
         scores = jnp.where(allowed, mm(keys, queries, NT), BLOCKED)
         return scores, mm(values, live, NT)
 
-    def finish(at, scores, prob_grad, keys, queries, live, base, to, accum_k, accum_v):
+    def finish(at, scores, prob_grad, keys, base, to, row0, grads_to, probs_to):
         top = jnp.max(scores, axis=0, keepdims=True)
         weights = jnp.exp2((scores - top) * exp_scale)
         total = jnp.sum(weights, axis=0, keepdims=True)
@@ -123,29 +135,20 @@
         out_dot = jnp.sum(probs_low.astype(F32) * prob_grad, axis=0, keepdims=True)
         score_grad = (probs * (prob_grad - out_dot)).astype(BF16)
         query_grad = mm(score_grad, keys, TN) * softmax_scale
-        place = pl.ds(pl.multiple_of(to + at * chunk, chunk), chunk)
-        dq32[place, :] = query_grad
-        dq_out[place, :] = query_grad.astype(BF16)
-        part_k = mm(score_grad, queries, NN)
-        part_v = mm(probs_low, live, NN)
-        if at == 0:
-            accum_k[...] = part_k
-            accum_v[...] = part_v
-        else:
-            accum_k[...] += part_k
-            accum_v[...] += part_v
-
-    load_qe.wait()
-    load_de.wait()
-    for at in range(chunks):
-        queries = q_s[at * chunk : (at + 1) * chunk]
-        live = do_s[at * chunk : (at + 1) * chunk]
-        keys = k_s[0:half]
-        scores, prob_grad = own_part(at, keys, v_s[0:half], queries, live, start_early)
-        finish(at, scores, prob_grad, keys, queries, live, start_early, early_q, acc_ke, acc_ve)
-
-    pl.semaphore_wait(barrier, nc + nh + nd - 3)
-
+        dq32[row0 + at * chunk : row0 + (at + 1) * chunk] = query_grad
+        dq_out[pl.ds(pl.multiple_of(to + at * chunk, chunk), chunk), :] = query_grad.astype(BF16)
+        lanes = slice(at * chunk, (at + 1) * chunk)
+        grads_to[:, lanes] = score_grad
+        probs_to[:, lanes] = probs_low
+
+    def rank_part(row0, to):
+        for g in range(group):
+            dqcat[pl.ds(to, half), g * 128 : (g + 1) * 128] = dq32[pl.ds(row0 + g, half, stride=group), :].astype(
+                BF16
+            )
+        rg_buf[here_h, :, pl.ds(to, half)] = mm(up_flat, dqcat[pl.ds(to, half), :], NT)
+
+    pl.semaphore_wait(barrier, len(near))
     kv_copies = [
         remote(ref.at[pl.ds(0, half)], ref.at[pl.ds(half, half)], kv_send.at[at], kv_recv.at[at], in_ctx(1))
         for at, ref in enumerate((k_s, v_s))
@@ -161,6 +164,16 @@
         k_s[half:rows] = k_s[0:half]
         v_s[half:rows] = v_s[0:half]
 
+    tell(relay_sems.at[0], [flip] + beside)
+
+    load_qe.wait()
+    load_de.wait()
+    for at in range(chunks):
+        place = slice(at * chunk, (at + 1) * chunk)
+        keys = k_s[0:half]
+        scores, prob_grad = own_part(at, keys, v_s[0:half], q_s[place], do_s[place], start_early)
+        finish(at, scores, prob_grad, keys, start_early, early_q, 0, sg_e, pr_e)
+
     def head_exchange(buf, sems):
         for step in far_first(nh):
             remote(buf.at[here_h], buf.at[here_h], sems.at[0], sems.at[1], in_head(step)).start()
@@ -168,7 +181,9 @@
     load_x.wait()
     load_at.wait()
     ri_buf[here_h] = mm(at_s[...], x_s[...], NT)
+    pl.semaphore_wait(relay_sems.at[0], 1 + len(beside))
     head_exchange(ri_buf, ri_sems)
+    tell(relay_sems.at[1], two_off)
 
     load_kl.wait()
     load_vl.wait()
@@ -185,6 +200,9 @@
     up_flat = jnp.concatenate(
         [u_s[...].astype(F32).reshape(rank, group, 128)[:, g, :] for g in range(group)], axis=1
     ).astype(BF16)
+    rank_part(0, early_m)
+    acc_ke[...] = mm(sg_e[...], q_s[0:hq], NN)
+    acc_ve[...] = mm(pr_e[...], do_s[0:hq], NN)
 
     @pl.when(is_shifted)
     def _():
@@ -193,19 +211,16 @@
 
     prev_seen = lax.broadcasted_iota(jnp.int32, (half, chunk), 0) < length - start_prev
     for at in range(chunks):
-        queries = q_s[hq + at * chunk : hq + (at + 1) * chunk]
-        live = do_s[hq + at * chunk : hq + (at + 1) * chunk]
-        prev_scores = jnp.where(prev_seen, mm(k_s[half:rows], queries, NT), BLOCKED)
+        place = slice(hq + at * chunk, hq + (at + 1) * chunk)
+        prev_scores = jnp.where(prev_seen, mm(k_s[half:rows], q_s[place], NT), BLOCKED)
         scores = jnp.concatenate([prev_scores, own_scores[at]], axis=0)
-        prob_grad = jnp.concatenate([mm(v_s[half:rows], live, NT), own_grads[at]], axis=0)
-        finish(
-            at, scores, prob_grad, k_s[half : rows + half], queries, live, start_late, late_q, acc_kl, acc_vl
-        )
-
-    for g in range(group):
-        dqcat[:, g * 128 : (g + 1) * 128] = dq32[pl.ds(g, rows, stride=group), :].astype(BF16)
-    rg_buf[here_h] = mm(up_flat, dqcat[...], NT)
+        prob_grad = jnp.concatenate([mm(v_s[half:rows], do_s[place], NT), own_grads[at]], axis=0)
+        finish(at, scores, prob_grad, k_s[half : rows + half], start_late, late_q, hq, sg_l, pr_l)
+
+    rank_part(hq, late_m)
     head_exchange(rg_buf, rg_sems)
+    acc_kl[...] = mm(sg_l[...], q_s[hq : 2 * hq], NN)
+    acc_vl[...] = mm(pr_l[...], do_s[hq : 2 * hq], NN)
 
     ret_copy = remote(ret_send, ret_recv, ret_sems.at[0], ret_sems.at[1], in_ctx(nc - 1))
 
@@ -241,6 +256,7 @@
 
     dkv_out[0, pl.ds(late_m, half), :] = (acc_kl[half:rows] * softmax_scale).astype(BF16)
     dkv_out[1, pl.ds(late_m, half), :] = acc_vl[half:rows].astype(BF16)
+    pl.semaphore_wait(relay_sems.at[1], len(two_off))
     send_over_ctx(up_a, up_asem, up_b, up_bsem)
 
     many(rg_buf, nh - 1, rg_sems.at[1]).wait()
@@ -325,6 +341,10 @@
             pltpu.VMEM((rows, group * width), BF16),
             pltpu.VMEM((hq // CHUNK, half, CHUNK), F32),
             pltpu.VMEM((hq // CHUNK, half, CHUNK), F32),
+            pltpu.VMEM((half, hq), BF16),
+            pltpu.VMEM((half, hq), BF16),
+            pltpu.VMEM((rows, hq), BF16),
+            pltpu.VMEM((rows, hq), BF16),
             pltpu.VMEM((half, width), F32),
             pltpu.VMEM((half, width), F32),
             pltpu.VMEM((rows, width), F32),
@@ -340,7 +360,8 @@
         ]
         * 2
         + [pltpu.SemaphoreType.DMA((12,))]
-        + [pair] * 9,
+        + [pair] * 9
+        + [pltpu.SemaphoreType.REGULAR((2,))],
         compiler_params=pltpu.CompilerParams(
             collective_id=0, has_side_effects=True, vmem_limit_bytes=40 * 1024 * 1024
         ),

time: 29.7 us -> 29 us (0.976); the launches traced: 29.3 us -> 28.9 us
  Pallas kernels: 28 us -> 27.6 us
    pallas_call x1, Pallas kernels: 27.1 us -> 26.7 us  [on_device(): pl.pallas_call(functools.partial(kernel, dims), out_shape=tuple((pltpu.VM...]
where the time goes in v5:
time: 29 us; the launch traced here: 28.9 us
  Pallas kernels  27.6 us (95%)
  between operations  1.29 us (4%)
    pallas_call x1, Pallas kernels, on_device(): pl.pallas_call(functools.partial(kernel, dims), out_shape=tuple((pltpu.VM...  26.7 us
    pallas_call x1, Pallas kernels, on_device(): pl.pallas_call(write_out, out_shape=(jax.ShapeDtypeStruct(*results[0]), j...  0.89 us

profile of v5, /device:TPU:1, one launch (start us, length us, event | category | flops | bytes accessed | tf_op | source)
XLA Modules:
  0.0 28.9 jit_solution(1861727678495942258)
XLA Ops:
  1.3 26.7 %attention_and_rank_gradients.1 = (bf16[2048,128]{1,0:T(8,128)(2,1)S(1)}, bf16[2,256,128]{2,1,0:T(8,128)(2,1)S(1)}, f32[8,1024]{1,0:T(8,128)S(1)}, f32[8,8,128]{2,1,0:T(8,128)S(1)}) custom-call(bf16[2048,128]{1,0:T(8,128)(2,1)} %bitcast.18, bf16[256,128]{1,0:T(8,128)(2,1)} %bitcast.21, bf16[256,128]{1,0:T(8,128)(2,1)} %bitcast.22, ...), custom_call_target="tpu_custom_call" | custom-call | tf_op jit(solution)/shard_map/attention_and_rank_gradients/pallas_call | solution.py:327
  28.0 0.9 %write_results.1 = (bf16[2048,128]{1,0:T(8,128)(2,1)}, bf16[256,128]{1,0:T(8,128)(2,1)}, bf16[256,128]{1,0:T(8,128)(2,1)}, f32[8,1024]{1,0:T(8,128)}, f32[8,8,128]{2,1,0:T(8,128)}) custom-call(bf16[2048,128]{1,0:T(8,128)(2,1)S(1)} %get-tuple-element.14.refs_0_, bf16[2,256,128]{2,1,0:T(8,128)(2,1)S(1)} %get-tuple-element.15.refs_1_, ...), custom_call_target="tpu_custom_call" | custom-call | tf_op jit(solution)/shard_map/write_results/pallas_call | solution.py:373
  (1 shorter events, 0.0 us)

commit v6 on v5

--- a/solution.py
+++ b/solution.py
@@ -10,7 +10,7 @@
 
 ADAPTER_SCALE = 2.0
 BLOCKED = -1e30
-CHUNK = 256
+CHUNK = 512
 MESH = pl.DeviceIdType.MESH
 F32 = jnp.float32
 BF16 = jnp.bfloat16
@@ -34,15 +34,16 @@
     q_s, do_s, x_s, at_s, u_s, k_s, v_s,
     dq32, dqcat, own_scores, own_grads, sg_e, pr_e, sg_l, pr_l,
     acc_ke, acc_ve, acc_kl, acc_vl, ret_send, ret_recv,
-    ri_buf, rg_buf, up_a, up_b, dn_a, dn_b,
+    ri_buf, rg_buf, up_p, up_a, up_b, up_c, dn_a, dn_b,
     load_sem, kv_send, kv_recv, ret_sems, ri_sems, rg_sems,
-    up_asem, up_bsem, dn_asem, dn_bsem, relay_sems,
+    up_asem, up_bsem, up_csem, dn_asem, dn_bsem, relay_sems,
 ):
     nd, nc, nh, half, group, rank = dims
     rows = 2 * half
     hq = half * group
     here_d, here_c, here_h = lax.axis_index("dp"), lax.axis_index("ctx"), lax.axis_index("head")
     is_shifted = here_h < nh // 2
+    core = lax.rem(here_d, 2)
     shifted = jnp.where(is_shifted, 1, 0)
     early = shifted * half
     late = (1 - shifted) * half
@@ -181,10 +182,6 @@
     load_x.wait()
     load_at.wait()
     ri_buf[here_h] = mm(at_s[...], x_s[...], NT)
-    pl.semaphore_wait(relay_sems.at[0], 1 + len(beside))
-    head_exchange(ri_buf, ri_sems)
-    tell(relay_sems.at[1], two_off)
-
     load_kl.wait()
     load_vl.wait()
     load_ql.wait()
@@ -203,6 +200,10 @@
     rank_part(0, early_m)
     acc_ke[...] = mm(sg_e[...], q_s[0:hq], NN)
     acc_ve[...] = mm(pr_e[...], do_s[0:hq], NN)
+    pl.semaphore_wait(relay_sems.at[0], 1 + len(beside))
+    head_exchange(ri_buf, ri_sems)
+    tell(relay_sems.at[1], two_off)
+
 
     @pl.when(is_shifted)
     def _():
@@ -245,6 +246,26 @@
                 onward.at[here_c], onward.at[here_c], onward_sems.at[0], onward_sems.at[1], in_ctx(step)
             ).start()
 
+    def send_halves_over_dp(total, part, recv, sems):
+        for at in range(2):
+            left = at * wide
+            part[at] = jnp.concatenate(
+                [total[:, left : left + wide // 2], total[:, left + wide // 2 : left + wide]], axis=0
+            ).astype(BF16)
+        recv[here_d] = part[core]
+        for step in range(nd - 1, 0, -1):
+            peer = in_dp(step)
+            remote(part.at[lax.rem(peer[0], 2)], recv.at[here_d], sems.at[0], sems.at[1], peer).start()
+
+    def swap_halves(recv, sems, both, both_sems):
+        many(recv, nc - 1, sems.at[1]).wait()
+        both[core] = jnp.sum(recv[...].astype(F32), axis=0)
+        copy = remote(
+            both.at[core], both.at[core], both_sems.at[0], both_sems.at[1], (here_d + 1 - 2 * core, here_c, here_h)
+        )
+        copy.start()
+        return copy
+
     def whole(recv, sems):
         many(recv, nc - 1, sems.at[1]).wait()
         total = jnp.sum(recv[...].astype(F32), axis=0)
@@ -252,16 +273,17 @@
 
     many(ri_buf, nh - 1, ri_sems.at[1]).wait()
     rank_input = jnp.sum(ri_buf[...], axis=0).astype(BF16)
-    send_over_dp(mm(rank_input, dqcat[...], NN) * ADAPTER_SCALE, up_a, up_asem)
-
-    dkv_out[0, pl.ds(late_m, half), :] = (acc_kl[half:rows] * softmax_scale).astype(BF16)
-    dkv_out[1, pl.ds(late_m, half), :] = acc_vl[half:rows].astype(BF16)
-    pl.semaphore_wait(relay_sems.at[1], len(two_off))
-    send_over_ctx(up_a, up_asem, up_b, up_bsem)
+    send_halves_over_dp(mm(rank_input, dqcat[...], NN) * ADAPTER_SCALE, up_p, up_a, up_asem)
 
     many(rg_buf, nh - 1, rg_sems.at[1]).wait()
     rank_grad = jnp.sum(rg_buf[...], axis=0).astype(BF16)
     send_over_dp(mm(rank_grad, x_s[...], NN) * ADAPTER_SCALE, dn_a, dn_asem)
+
+    pl.semaphore_wait(relay_sems.at[1], len(two_off))
+    send_over_ctx(up_a, up_asem, up_b, up_bsem)
+
+    dkv_out[0, pl.ds(late_m, half), :] = (acc_kl[half:rows] * softmax_scale).astype(BF16)
+    dkv_out[1, pl.ds(late_m, half), :] = acc_vl[half:rows].astype(BF16)
 
     @pl.when(is_shifted)
     def _():
@@ -277,7 +299,11 @@
         dkv_out[1, pl.ds(early_m, half), :] = (acc_ve[...] + acc_vl[0:half]).astype(BF16)
 
     send_over_ctx(dn_a, dn_asem, dn_b, dn_bsem)
-    up_whole = whole(up_b, up_bsem)
+    up_swap = swap_halves(up_b, up_bsem, up_c, up_csem)
+    up_swap.wait()
+    up_whole = jnp.concatenate(
+        [up_c[at, rank * row : rank * (row + 1)] for at in range(2) for row in range(2)], axis=1
+    )
     for g in range(group):
         up_out[:, g, :] = up_whole[:, g * 128 : (g + 1) * 128]
     for buf, count, sem in (
@@ -309,6 +335,7 @@
     vmem = pl.BlockSpec(memory_space=pltpu.VMEM)
     pair = pltpu.SemaphoreType.DMA((2,))
     packed = (2 * rank, group * width // 2)
+    halved = (2 * rank, group * width // 4)
     results = (
         ((rows * group, width), BF16),
         ((2, rows, width), BF16),
@@ -355,12 +382,15 @@
             pltpu.VMEM((nh, rank, rows), F32),
         ]
         + [
+            pltpu.VMEM((2,) + halved, BF16),
+            pltpu.VMEM((nd,) + halved, BF16),
+            pltpu.VMEM((nc,) + halved, BF16),
+            pltpu.VMEM((2,) + halved, F32),
             pltpu.VMEM((nd,) + packed, BF16),
             pltpu.VMEM((nc,) + packed, BF16),
         ]
-        * 2
         + [pltpu.SemaphoreType.DMA((12,))]
-        + [pair] * 9
+        + [pair] * 10
         + [pltpu.SemaphoreType.REGULAR((2,))],
         compiler_params=pltpu.CompilerParams(
             collective_id=0, has_side_effects=True, vmem_limit_bytes=40 * 1024 * 1024

time: 29 us -> 27.5 us (0.948)
  Pallas kernels: 27.6 us -> 25.9 us
    pallas_call x1, Pallas kernels: 26.7 us -> 25 us  [on_device(): pl.pallas_call(functools.partial(kernel, dims), out_shape=tuple((pltpu.VM...]
where the time goes in v6:
time: 27.5 us; the launch traced here: 27.2 us
  Pallas kernels  25.9 us (94%)
  between operations  1.29 us (5%)
    pallas_call x1, Pallas kernels, on_device(): pl.pallas_call(functools.partial(kernel, dims), out_shape=tuple((pltpu.VM...  25 us
    pallas_call x1, Pallas kernels, on_device(): pl.pallas_call(write_out, out_shape=(jax.ShapeDtypeStruct(*results[0]), j...  0.89 us

profile of v6, /device:TPU:1, one launch (start us, length us, event | category | flops | bytes accessed | tf_op | source)
XLA Modules:
  0.0 27.2 jit_solution(7287108442320582690)
XLA Ops:
  1.3 25.0 %attention_and_rank_gradients.1 = (bf16[2048,128]{1,0:T(8,128)(2,1)S(1)}, bf16[2,256,128]{2,1,0:T(8,128)(2,1)S(1)}, f32[8,1024]{1,0:T(8,128)S(1)}, f32[8,8,128]{2,1,0:T(8,128)S(1)}) custom-call(bf16[2048,128]{1,0:T(8,128)(2,1)} %bitcast.18, bf16[256,128]{1,0:T(8,128)(2,1)} %bitcast.21, bf16[256,128]{1,0:T(8,128)(2,1)} %bitcast.22, ...), custom_call_target="tpu_custom_call" | custom-call | tf_op jit(solution)/shard_map/attention_and_rank_gradients/pallas_call | solution.py:354
  26.3 0.9 %write_results.1 = (bf16[2048,128]{1,0:T(8,128)(2,1)}, bf16[256,128]{1,0:T(8,128)(2,1)}, bf16[256,128]{1,0:T(8,128)(2,1)}, f32[8,1024]{1,0:T(8,128)}, f32[8,8,128]{2,1,0:T(8,128)}) custom-call(bf16[2048,128]{1,0:T(8,128)(2,1)S(1)} %get-tuple-element.14.refs_0_, bf16[2,256,128]{2,1,0:T(8,128)(2,1)S(1)} %get-tuple-element.15.refs_1_, ...), custom_call_target="tpu_custom_call" | custom-call | tf_op jit(solution)/shard_map/write_results/pallas_call | solution.py:403
  (1 shorter events, 0.0 us)

commit v7 on v6

--- a/solution.py
+++ b/solution.py
@@ -10,7 +10,7 @@
 
 ADAPTER_SCALE = 2.0
 BLOCKED = -1e30
-CHUNK = 512
+CHUNK = 1024
 MESH = pl.DeviceIdType.MESH
 F32 = jnp.float32
 BF16 = jnp.bfloat16
@@ -32,7 +32,7 @@
     q_in, k_in, v_in, do_in, x_in, at_in, u_in, len_in,
     dq_out, dkv_out, down_out, up_out,
     q_s, do_s, x_s, at_s, u_s, k_s, v_s,
-    dq32, dqcat, own_scores, own_grads, sg_e, pr_e, sg_l, pr_l,
+    dq32, dqcat, own_scores, own_grads, sg_e, pr_e, sg_l, pr_l, fold,
     acc_ke, acc_ve, acc_kl, acc_vl, ret_send, ret_recv,
     ri_buf, rg_buf, up_p, up_a, up_b, up_c, dn_a, dn_b,
     load_sem, kv_send, kv_recv, ret_sems, ri_sems, rg_sems,
@@ -60,8 +60,19 @@
     def in_ctx(step):
         return (here_d, lax.rem(here_c + step, nc), here_h)
 
-    def in_dp(step):
-        return (lax.rem(here_d + step, nd), here_c, here_h)
+    def dp_peers():
+        moves = [(x, c) for x in range(nd // 2 - 1, -1, -1) for c in (1, 0) if (x, c) != (0, 0)]
+        return [
+            (lax.rem(here_d // 2 + x, nd // 2) * 2 + lax.rem(core + c, 2), here_c, here_h) for x, c in moves
+        ]
+
+    def head_peers():
+        ny, side = nh // 2, lax.rem(here_h, 2)
+        moves = [(y, x) for y in range(ny) for x in range(2) if (y, x) != (0, 0)]
+        moves.sort(key=lambda move: -(min(move[0], ny - move[0]) + 2 * move[1]))
+        return [
+            (here_d, here_c, lax.rem(here_h // 2 + y, ny) * 2 + lax.rem(side + x, 2)) for y, x in moves
+        ]
 
     flip = (here_d, here_c, here_h + 1 - 2 * lax.rem(here_h, 2))
     beside = [in_ctx(step) for step in sorted({1, nc - 1})]
@@ -69,7 +80,7 @@
     near = (
         [flip]
         + [in_head(step) for step in sorted({2, 4, nh - 2}) if 0 < step < nh]
-        + [in_dp(step) for step in range(nd - 1, 0, -1)]
+        + dp_peers()
         + beside
     )
 
@@ -125,7 +136,7 @@
         scores = jnp.where(allowed, mm(keys, queries, NT), BLOCKED)
         return scores, mm(values, live, NT)
 
-    def finish(at, scores, prob_grad, keys, base, to, row0, grads_to, probs_to):
+    def finish(at, scores, prob_grad, base, grads_to, probs_to):
         top = jnp.max(scores, axis=0, keepdims=True)
         weights = jnp.exp2((scores - top) * exp_scale)
         total = jnp.sum(weights, axis=0, keepdims=True)
@@ -135,19 +146,21 @@
         probs_low = probs.astype(BF16)
         out_dot = jnp.sum(probs_low.astype(F32) * prob_grad, axis=0, keepdims=True)
         score_grad = (probs * (prob_grad - out_dot)).astype(BF16)
+        lanes = slice(at * chunk, (at + 1) * chunk)
+        grads_to[:, lanes] = score_grad
+        probs_to[:, lanes] = probs_low
+        return score_grad
+
+    def query_part(at, score_grad, keys, to, row0):
         query_grad = mm(score_grad, keys, TN) * softmax_scale
         dq32[row0 + at * chunk : row0 + (at + 1) * chunk] = query_grad
         dq_out[pl.ds(pl.multiple_of(to + at * chunk, chunk), chunk), :] = query_grad.astype(BF16)
-        lanes = slice(at * chunk, (at + 1) * chunk)
-        grads_to[:, lanes] = score_grad
-        probs_to[:, lanes] = probs_low
-
-    def rank_part(row0, to):
+
+    def by_head(row0, to):
         for g in range(group):
             dqcat[pl.ds(to, half), g * 128 : (g + 1) * 128] = dq32[pl.ds(row0 + g, half, stride=group), :].astype(
                 BF16
             )
-        rg_buf[here_h, :, pl.ds(to, half)] = mm(up_flat, dqcat[pl.ds(to, half), :], NT)
 
     pl.semaphore_wait(barrier, len(near))
     kv_copies = [
@@ -173,11 +186,11 @@
         place = slice(at * chunk, (at + 1) * chunk)
         keys = k_s[0:half]
         scores, prob_grad = own_part(at, keys, v_s[0:half], q_s[place], do_s[place], start_early)
-        finish(at, scores, prob_grad, keys, start_early, early_q, 0, sg_e, pr_e)
+        query_part(at, finish(at, scores, prob_grad, start_early, sg_e, pr_e), keys, early_q, 0)
 
     def head_exchange(buf, sems):
-        for step in far_first(nh):
-            remote(buf.at[here_h], buf.at[here_h], sems.at[0], sems.at[1], in_head(step)).start()
+        for peer in head_peers():
+            remote(buf.at[here_h], buf.at[here_h], sems.at[0], sems.at[1], peer).start()
 
     load_x.wait()
     load_at.wait()
@@ -194,10 +207,16 @@
         own_scores[at] = scores
         own_grads[at] = prob_grad
     load_u.wait()
-    up_flat = jnp.concatenate(
-        [u_s[...].astype(F32).reshape(rank, group, 128)[:, g, :] for g in range(group)], axis=1
+    up_heads = [u_s[...].astype(F32).reshape(rank, group, 128)[:, g, :] for g in range(group)]
+    up_flat = jnp.concatenate(up_heads, axis=1).astype(BF16)
+    up_tall = jnp.concatenate(up_heads, axis=0).astype(BF16)
+    by_head(0, early_m)
+    rg_buf[here_h, :, pl.ds(early_m, half)] = mm(up_flat, dqcat[pl.ds(early_m, half), :], NT)
+    fold[...] = jnp.where(
+        lax.broadcasted_iota(jnp.int32, (hq, half), 0) // group == lax.broadcasted_iota(jnp.int32, (hq, half), 1),
+        1.0,
+        0.0,
     ).astype(BF16)
-    rank_part(0, early_m)
     acc_ke[...] = mm(sg_e[...], q_s[0:hq], NN)
     acc_ve[...] = mm(pr_e[...], do_s[0:hq], NN)
     pl.semaphore_wait(relay_sems.at[0], 1 + len(beside))
@@ -210,16 +229,29 @@
         for copy in kv_copies:
             copy.wait()
 
+    key_up = (mm(up_tall, k_s[half : rows + half], NT) * softmax_scale).astype(BF16)
+    lane_head = lax.rem(lax.broadcasted_iota(jnp.int32, (rank, chunk), 1), group)
     prev_seen = lax.broadcasted_iota(jnp.int32, (half, chunk), 0) < length - start_prev
+    folded = []
     for at in range(chunks):
         place = slice(hq + at * chunk, hq + (at + 1) * chunk)
         prev_scores = jnp.where(prev_seen, mm(k_s[half:rows], q_s[place], NT), BLOCKED)
         scores = jnp.concatenate([prev_scores, own_scores[at]], axis=0)
         prob_grad = jnp.concatenate([mm(v_s[half:rows], do_s[place], NT), own_grads[at]], axis=0)
-        finish(at, scores, prob_grad, k_s[half : rows + half], start_late, late_q, hq, sg_l, pr_l)
-
-    rank_part(hq, late_m)
+        all_heads = mm(key_up, finish(at, scores, prob_grad, start_late, sg_l, pr_l), NN)
+        own_head = jnp.zeros((rank, chunk), F32)
+        for g in range(group):
+            own_head += jnp.where(lane_head == g, all_heads[rank * g : rank * (g + 1)], 0.0)
+        rest = own_head - own_head.astype(BF16).astype(F32)
+        both = jnp.concatenate([own_head, rest], axis=0).astype(BF16)
+        folded.append(mm(both, fold[at * chunk : (at + 1) * chunk], NN))
+
+    folded = sum(folded)
+    rg_buf[here_h, :, pl.ds(late_m, half)] = folded[:rank] + folded[rank:]
     head_exchange(rg_buf, rg_sems)
+    for at in range(chunks):
+        query_part(at, sg_l[:, at * chunk : (at + 1) * chunk], k_s[half : rows + half], late_q, hq)
+    by_head(hq, late_m)
     acc_kl[...] = mm(sg_l[...], q_s[hq : 2 * hq], NN)
     acc_vl[...] = mm(pr_l[...], do_s[hq : 2 * hq], NN)
 
@@ -235,16 +267,19 @@
 
     def send_over_dp(total, recv, sems):
         recv[here_d] = jnp.concatenate([total[:, :wide], total[:, wide:]], axis=0).astype(BF16)
-        for step in range(nd - 1, 0, -1):
-            remote(recv.at[here_d], recv.at[here_d], sems.at[0], sems.at[1], in_dp(step)).start()
+        for peer in dp_peers():
+            remote(recv.at[here_d], recv.at[here_d], sems.at[0], sems.at[1], peer).start()
 
     def send_over_ctx(recv, sems, onward, onward_sems):
         many(recv, nd - 1, sems.at[1]).wait()
         onward[here_c] = jnp.sum(recv[...].astype(F32), axis=0).astype(BF16)
-        for step in far_first(nc):
-            remote(
-                onward.at[here_c], onward.at[here_c], onward_sems.at[0], onward_sems.at[1], in_ctx(step)
-            ).start()
+        later = sorted(range(nc - 1, nc // 2 - 1, -1), key=lambda to: min(nc - to, to - nc // 2 + 1))
+        for to in list(range(nc // 2)) + later:
+            @pl.when(here_c != to)
+            def _():
+                remote(
+                    onward.at[here_c], onward.at[here_c], onward_sems.at[0], onward_sems.at[1], (here_d, to, here_h)
+                ).start()
 
     def send_halves_over_dp(total, part, recv, sems):
         for at in range(2):
@@ -253,8 +288,7 @@
                 [total[:, left : left + wide // 2], total[:, left + wide // 2 : left + wide]], axis=0
             ).astype(BF16)
         recv[here_d] = part[core]
-        for step in range(nd - 1, 0, -1):
-            peer = in_dp(step)
+        for peer in dp_peers():
             remote(part.at[lax.rem(peer[0], 2)], recv.at[here_d], sems.at[0], sems.at[1], peer).start()
 
     def swap_halves(recv, sems, both, both_sems):
@@ -285,6 +319,8 @@
     dkv_out[0, pl.ds(late_m, half), :] = (acc_kl[half:rows] * softmax_scale).astype(BF16)
     dkv_out[1, pl.ds(late_m, half), :] = acc_vl[half:rows].astype(BF16)
 
+    send_over_ctx(dn_a, dn_asem, dn_b, dn_bsem)
+
     @pl.when(is_shifted)
     def _():
         ret_copy.wait()
@@ -298,7 +334,6 @@
         dkv_out[0, pl.ds(early_m, half), :] = ((acc_ke[...] + acc_kl[0:half]) * softmax_scale).astype(BF16)
         dkv_out[1, pl.ds(early_m, half), :] = (acc_ve[...] + acc_vl[0:half]).astype(BF16)
 
-    send_over_ctx(dn_a, dn_asem, dn_b, dn_bsem)
     up_swap = swap_halves(up_b, up_bsem, up_c, up_csem)
     up_swap.wait()
     up_whole = jnp.concatenate(
@@ -372,6 +407,7 @@
             pltpu.VMEM((half, hq), BF16),
             pltpu.VMEM((rows, hq), BF16),
             pltpu.VMEM((rows, hq), BF16),
+            pltpu.VMEM((hq, half), BF16),
             pltpu.VMEM((half, width), F32),
             pltpu.VMEM((half, width), F32),
             pltpu.VMEM((rows, width), F32),

time: 27.5 us -> 27.3 us (level)
  no operation moved by 1% of the time
where the time goes in v7:
time: 27.3 us; the launch traced here: 27.2 us
  Pallas kernels  25.9 us (95%)
  between operations  1.29 us (5%)
    pallas_call x1, Pallas kernels, on_device(): pl.pallas_call(functools.partial(kernel, dims), out_shape=tuple((pltpu.VM...  25 us
    pallas_call x1, Pallas kernels, on_device(): pl.pallas_call(write_out, out_shape=(jax.ShapeDtypeStruct(*results[0]), j...  0.89 us

profile of v7, /device:TPU:1, one launch (start us, length us, event | category | flops | bytes accessed | tf_op | source)
XLA Modules:
  0.0 27.2 jit_solution(8114443242354812705)
XLA Ops:
  1.3 25.0 %attention_and_rank_gradients.1 = (bf16[2048,128]{1,0:T(8,128)(2,1)S(1)}, bf16[2,256,128]{2,1,0:T(8,128)(2,1)S(1)}, f32[8,1024]{1,0:T(8,128)S(1)}, f32[8,8,128]{2,1,0:T(8,128)S(1)}) custom-call(bf16[2048,128]{1,0:T(8,128)(2,1)} %bitcast.18, bf16[256,128]{1,0:T(8,128)(2,1)} %bitcast.21, bf16[256,128]{1,0:T(8,128)(2,1)} %bitcast.22, ...), custom_call_target="tpu_custom_call" | custom-call | tf_op jit(solution)/shard_map/attention_and_rank_gradients/pallas_call | solution.py:389
  26.3 0.9 %write_results.1 = (bf16[2048,128]{1,0:T(8,128)(2,1)}, bf16[256,128]{1,0:T(8,128)(2,1)}, bf16[256,128]{1,0:T(8,128)(2,1)}, f32[8,1024]{1,0:T(8,128)}, f32[8,8,128]{2,1,0:T(8,128)}) custom-call(bf16[2048,128]{1,0:T(8,128)(2,1)S(1)} %get-tuple-element.14.refs_0_, bf16[2,256,128]{2,1,0:T(8,128)(2,1)S(1)} %get-tuple-element.15.refs_1_, ...), custom_call_target="tpu_custom_call" | custom-call | tf_op jit(solution)/shard_map/write_results/pallas_call | solution.py:439
  (1 shorter events, 0.0 us)

commit v8 on v6

--- a/solution.py
+++ b/solution.py
@@ -60,8 +60,19 @@
     def in_ctx(step):
         return (here_d, lax.rem(here_c + step, nc), here_h)
 
-    def in_dp(step):
-        return (lax.rem(here_d + step, nd), here_c, here_h)
+    def dp_peers():
+        moves = [(x, c) for x in range(nd // 2 - 1, -1, -1) for c in (1, 0) if (x, c) != (0, 0)]
+        return [
+            (lax.rem(here_d // 2 + x, nd // 2) * 2 + lax.rem(core + c, 2), here_c, here_h) for x, c in moves
+        ]
+
+    def head_peers():
+        ny, side = nh // 2, lax.rem(here_h, 2)
+        moves = [(y, x) for y in range(ny) for x in range(2) if (y, x) != (0, 0)]
+        moves.sort(key=lambda move: -(min(move[0], ny - move[0]) + 2 * move[1]))
+        return [
+            (here_d, here_c, lax.rem(here_h // 2 + y, ny) * 2 + lax.rem(side + x, 2)) for y, x in moves
+        ]
 
     flip = (here_d, here_c, here_h + 1 - 2 * lax.rem(here_h, 2))
     beside = [in_ctx(step) for step in sorted({1, nc - 1})]
@@ -69,7 +80,7 @@
     near = (
         [flip]
         + [in_head(step) for step in sorted({2, 4, nh - 2}) if 0 < step < nh]
-        + [in_dp(step) for step in range(nd - 1, 0, -1)]
+        + dp_peers()
         + beside
     )
 
@@ -176,8 +187,8 @@
         finish(at, scores, prob_grad, keys, start_early, early_q, 0, sg_e, pr_e)
 
     def head_exchange(buf, sems):
-        for step in far_first(nh):
-            remote(buf.at[here_h], buf.at[here_h], sems.at[0], sems.at[1], in_head(step)).start()
+        for peer in head_peers():
+            remote(buf.at[here_h], buf.at[here_h], sems.at[0], sems.at[1], peer).start()
 
     load_x.wait()
     load_at.wait()
@@ -235,16 +246,19 @@
 
     def send_over_dp(total, recv, sems):
         recv[here_d] = jnp.concatenate([total[:, :wide], total[:, wide:]], axis=0).astype(BF16)
-        for step in range(nd - 1, 0, -1):
-            remote(recv.at[here_d], recv.at[here_d], sems.at[0], sems.at[1], in_dp(step)).start()
+        for peer in dp_peers():
+            remote(recv.at[here_d], recv.at[here_d], sems.at[0], sems.at[1], peer).start()
 
     def send_over_ctx(recv, sems, onward, onward_sems):
         many(recv, nd - 1, sems.at[1]).wait()
         onward[here_c] = jnp.sum(recv[...].astype(F32), axis=0).astype(BF16)
-        for step in far_first(nc):
-            remote(
-                onward.at[here_c], onward.at[here_c], onward_sems.at[0], onward_sems.at[1], in_ctx(step)
-            ).start()
+        later = sorted(range(nc - 1, nc // 2 - 1, -1), key=lambda to: min(nc - to, to - nc // 2 + 1))
+        for to in list(range(nc // 2)) + later:
+            @pl.when(here_c != to)
+            def _():
+                remote(
+                    onward.at[here_c], onward.at[here_c], onward_sems.at[0], onward_sems.at[1], (here_d, to, here_h)
+                ).start()
 
     def send_halves_over_dp(total, part, recv, sems):
         for at in range(2):
@@ -253,8 +267,7 @@
                 [total[:, left : left + wide // 2], total[:, left + wide // 2 : left + wide]], axis=0
             ).astype(BF16)
         recv[here_d] = part[core]
-        for step in range(nd - 1, 0, -1):
-            peer = in_dp(step)
+        for peer in dp_peers():
             remote(part.at[lax.rem(peer[0], 2)], recv.at[here_d], sems.at[0], sems.at[1], peer).start()
 
     def swap_halves(recv, sems, both, both_sems):
@@ -285,6 +298,8 @@
     dkv_out[0, pl.ds(late_m, half), :] = (acc_kl[half:rows] * softmax_scale).astype(BF16)
     dkv_out[1, pl.ds(late_m, half), :] = acc_vl[half:rows].astype(BF16)
 
+    send_over_ctx(dn_a, dn_asem, dn_b, dn_bsem)
+
     @pl.when(is_shifted)
     def _():
         ret_copy.wait()
@@ -298,7 +313,6 @@
         dkv_out[0, pl.ds(early_m, half), :] = ((acc_ke[...] + acc_kl[0:half]) * softmax_scale).astype(BF16)
         dkv_out[1, pl.ds(early_m, half), :] = (acc_ve[...] + acc_vl[0:half]).astype(BF16)
 
-    send_over_ctx(dn_a, dn_asem, dn_b, dn_bsem)
     up_swap = swap_halves(up_b, up_bsem, up_c, up_csem)
     up_swap.wait()
     up_whole = jnp.concatenate(

time: 27.5 us -> 27.3 us (level)
  no operation moved by 1% of the time
where the time goes in v8:
time: 27.3 us; the launch traced here: 27.2 us
  Pallas kernels  25.9 us (95%)
  between operations  1.29 us (5%)
    pallas_call x1, Pallas kernels, on_device(): pl.pallas_call(functools.partial(kernel, dims), out_shape=tuple((pltpu.VM...  25 us
    pallas_call x1, Pallas kernels, on_device(): pl.pallas_call(write_out, out_shape=(jax.ShapeDtypeStruct(*results[0]), j...  0.89 us

profile of v8, /device:TPU:1, one launch (start us, length us, event | category | flops | bytes accessed | tf_op | source)
XLA Modules:
  0.0 27.2 jit_solution(3863189201140954304)
XLA Ops:
  1.3 25.0 %attention_and_rank_gradients.1 = (bf16[2048,128]{1,0:T(8,128)(2,1)S(1)}, bf16[2,256,128]{2,1,0:T(8,128)(2,1)S(1)}, f32[8,1024]{1,0:T(8,128)S(1)}, f32[8,8,128]{2,1,0:T(8,128)S(1)}) custom-call(bf16[2048,128]{1,0:T(8,128)(2,1)} %bitcast.18, bf16[256,128]{1,0:T(8,128)(2,1)} %bitcast.21, bf16[256,128]{1,0:T(8,128)(2,1)} %bitcast.22, ...), custom_call_target="tpu_custom_call" | custom-call | tf_op jit(solution)/shard_map/attention_and_rank_gradients/pallas_call | solution.py:368
  26.3 0.9 %write_results.1 = (bf16[2048,128]{1,0:T(8,128)(2,1)}, bf16[256,128]{1,0:T(8,128)(2,1)}, bf16[256,128]{1,0:T(8,128)(2,1)}, f32[8,1024]{1,0:T(8,128)}, f32[8,8,128]{2,1,0:T(8,128)}) custom-call(bf16[2048,128]{1,0:T(8,128)(2,1)S(1)} %get-tuple-element.14.refs_0_, bf16[2,256,128]{2,1,0:T(8,128)(2,1)S(1)} %get-tuple-element.15.refs_1_, ...), custom_call_target="tpu_custom_call" | custom-call | tf_op jit(solution)/shard_map/write_results/pallas_call | solution.py:417
  (1 shorter events, 0.0 us)
